TPU v7x, 256 devices: a whole 4x4x8 slice. The times are simulated.
256 devices in a mesh: blk: 64 (over x, z, y_lo), lat: 4 (over y_hi, core).
Axes of the slice: x: 4, y: 4 (y_hi: 2, y_lo: 2; y = y_hi * 2 + y_lo), z: 8, core: 2. Of those that a mesh axis runs over, the one named last changes fastest.
Arguments:
- displacement: float32 [3, 5, 5, 5, 64, 8, 128], P(None, None, None, None, 'blk', 'lat'), may hold values from -6 to 6
- velocity: float32 [3, 5, 5, 5, 64, 8, 128], P(None, None, None, None, 'blk', 'lat'), may hold values from -6 to 6
- rigidity: float32 [5, 5, 5, 64, 8, 128], P(None, None, None, 'blk', 'lat'), may hold values from 0.5 to 2
- density: float32 [5, 5, 5, 64, 8, 128], P(None, None, None, 'blk', 'lat'), may hold values from 0.5 to 2
- history: float32 [256, 63, 3, 128], P(('blk', 'lat')), may hold values from -0.12 to 0.12
- kernel: float32 [64, 3, 3, 128], replicated, may hold values from -0.4375 to 0.4375
- owner_order: int32 [256], replicated, may hold values from 0 to 255, each once
- rigid_offset: float32 [3], replicated, may hold values from -1.8 to 1.8
- rigid_velocity: float32 [3], replicated, may hold values from -6 to 6
Outputs:
- new_displacement: float32 [3, 5, 5, 5, 64, 8, 128], P(None, None, None, None, 'blk', 'lat')
- new_velocity: float32 [3, 5, 5, 5, 64, 8, 128], P(None, None, None, None, 'blk', 'lat')
- new_history: float32 [256, 63, 3, 128], P(('blk', 'lat'))
- new_offset: float32 [3], replicated
- new_rigid_velocity: float32 [3], replicated
Inputs may be any that keep to these rules, and one draw needn't show every extreme that they name: owner_order names every column 0 to 255 once; row j of history belongs to column owner_order[j].
All inputs are finite; a program needn't handle non-finite values.
Results may differ from a plain program's by a relative error of at most 0.0003.
Values sent between devices are 32-bit elements; how exact they have to be, the bound alone decides.
A program may use at most 64 MiB of HBM per device.

v0:
```python
import functools
import math

import jax
import jax.numpy as jnp
import numpy as np
from jax import lax
from jax.sharding import Mesh
from jax.sharding import PartitionSpec as P

STEPS = 3
BLK = ("blk_0", "blk_1", "blk_2")
LAT = ("lat_0", "lat_1")
BLK_LAT = ("blk_0", "blk_1", "blk_2", "lat_0", "lat_1")


pole_gap = 0.1
time_step = 0.03
rigid_gain = 20.0
coupling = 1.0
highest = lax.Precision.HIGHEST


def with_halo(block, sides, width, periodic):
    for axis, dim in sides:
        count = lax.axis_size(axis)
        forward = [(i, i + 1) for i in range(count - 1)]
        if periodic:
            forward.append((count - 1, 0))
        backward = [(target, source) for source, target in forward]
        low = lax.ppermute(
            lax.slice_in_dim(block, block.shape[dim] - width, None, axis=dim), axis, forward
        )
        high = lax.ppermute(lax.slice_in_dim(block, 0, width, axis=dim), axis, backward)
        block = jnp.concatenate([low, block, high], axis=dim)
    return block


def cut_along(shard, dim, length):
    lengths = shard.shape
    parts = shard.reshape(*lengths[:dim], length, lengths[dim] // length, *lengths[dim + 1 :])
    return jnp.moveaxis(parts, dim, 0)


def sum_at_owner(shard, axis, dim):
    parts = cut_along(shard, dim, lax.axis_size(axis))
    arrived = lax.all_to_all(parts, axis, split_axis=0, concat_axis=0, tiled=True)
    return arrived.sum(axis=0)


def over_axes(shard, axes):
    return functools.reduce(lax.psum, axes, shard)


def node_tables():
    points = np.array([-1.0, -math.sqrt(3.0 / 7.0), 0.0, math.sqrt(3.0 / 7.0), 1.0])
    weights = np.array([0.1, 49.0 / 90.0, 32.0 / 45.0, 49.0 / 90.0, 0.1])
    products = np.array(
        [
            np.prod([points[row_at] - points[others] for others in range(5) if others != row_at])
            for row_at in range(5)
        ]
    )
    slopes = np.zeros((5, 5))
    for row_at in range(5):
        for col_at in range(5):
            if row_at == col_at:
                slopes[row_at, col_at] = sum(
                    (
                        1.0 / (points[row_at] - points[others])
                        for others in range(5)
                        if others != row_at
                    )
                )
            else:
                slopes[row_at, col_at] = (
                    products[row_at] / products[col_at] / (points[row_at] - points[col_at])
                )
    return (points, weights, slopes)


def node_volume():
    points, weights, slopes = node_tables()
    node_weight = jnp.asarray(weights, dtype=jnp.float32)
    volume = node_weight[:, None, None] * node_weight[None, :, None] * node_weight[None, None, :]
    return volume[:, :, :, None, None, None]


def stiffness(values, rigidity):
    points, weights, slopes = node_tables()
    deriv = jnp.asarray(slopes, dtype=jnp.float32)
    scaled = (node_volume() * rigidity)[None]
    first_dir = jnp.einsum("ia,kabcxyz->kibcxyz", deriv, values, precision=highest) * scaled
    second_dir = jnp.einsum("jb,kabcxyz->kajcxyz", deriv, values, precision=highest) * scaled
    third_dir = jnp.einsum("lc,kabcxyz->kablxyz", deriv, values, precision=highest) * scaled
    result = jnp.einsum("ia,kibcxyz->kabcxyz", deriv, first_dir, precision=highest)
    result = result + jnp.einsum("jb,kajcxyz->kabcxyz", deriv, second_dir, precision=highest)
    return result + jnp.einsum("lc,kablxyz->kabcxyz", deriv, third_dir, precision=highest)


def join_faces(lower, upper, before_first, after_last, axis):
    count = lower.shape[axis]
    earlier = jnp.concatenate(
        (before_first, lax.slice_in_dim(upper, 0, count - 1, axis=axis)), axis=axis
    )
    later = jnp.concatenate((lax.slice_in_dim(lower, 1, count, axis=axis), after_last), axis=axis)
    return (lower + earlier, upper + later)


def assemble(forces):
    lower, upper = (forces[:, 0], forces[:, 4])
    count = lower.shape[3]
    paired = jnp.concatenate((lower, upper), axis=3)
    widened = with_halo(paired, ((BLK, 3),), 1, True)
    lower, upper = join_faces(
        lower,
        upper,
        lax.slice_in_dim(widened, 0, 1, axis=3),
        lax.slice_in_dim(widened, 3, 4, axis=3),
        3,
    )
    forces = forces.at[:, 0].set(lower).at[:, 4].set(upper)
    lower, upper = (forces[:, :, 0], forces[:, :, 4])
    count = lower.shape[4]
    paired = jnp.concatenate(
        (lax.slice_in_dim(lower, 0, 1, axis=4), lax.slice_in_dim(upper, count - 1, count, axis=4)),
        axis=4,
    )
    widened = with_halo(paired, ((LAT, 4),), 1, False)
    lower, upper = join_faces(
        lower,
        upper,
        lax.slice_in_dim(widened, 0, 1, axis=4),
        lax.slice_in_dim(widened, 3, 4, axis=4),
        4,
    )
    forces = forces.at[:, :, 0].set(lower).at[:, :, 4].set(upper)
    lower, upper = (forces[:, :, :, 0], forces[:, :, :, 4])
    empty = jnp.zeros_like(lax.slice_in_dim(lower, 0, 1, axis=5))
    lower, upper = join_faces(lower, upper, empty, empty, 5)
    return forces.at[:, :, :, 0].set(lower).at[:, :, :, 4].set(upper)


def interface_grid(row_first, row_count, col_first, col_count, lat_elems, lon_elems):
    points, weights, slopes = node_tables()
    nodes = jnp.asarray(points, dtype=jnp.float32)
    node_weight = jnp.asarray(weights, dtype=jnp.float32)
    theta_step = (math.pi - 2.0 * pole_gap) / lat_elems
    phi_step = 2.0 * math.pi / lon_elems
    row_elem = (row_first + jnp.arange(5 * row_count, dtype=jnp.int32) // 5).astype(jnp.float32)
    col_elem = (col_first + jnp.arange(5 * col_count, dtype=jnp.int32) // 5).astype(jnp.float32)
    colatitude = pole_gap + (row_elem + 0.5 * (1.0 + jnp.tile(nodes, row_count))) * theta_step
    longitude = (col_elem + 0.5 * (1.0 + jnp.tile(nodes, col_count))) * phi_step
    row_weight = jnp.tile(node_weight, row_count)
    col_weight = jnp.tile(node_weight, col_count)
    area_weight = (
        0.25
        * theta_step
        * phi_step
        * (row_weight * jnp.sin(colatitude))[:, None]
        * col_weight[None, :]
    )
    face_weight = row_weight[:, None] * col_weight[None, :]
    return (colatitude, longitude, area_weight, face_weight)


def rotation(colatitude, longitude):
    sin_theta = jnp.sin(colatitude)[:, None]
    cos_theta = jnp.cos(colatitude)[:, None]
    sin_phi = jnp.sin(longitude)[None, :]
    cos_phi = jnp.cos(longitude)[None, :]
    filled = jnp.ones((colatitude.shape[0], longitude.shape[0]), jnp.float32)
    radial = (sin_theta * cos_phi, sin_theta * sin_phi, cos_theta * filled)
    polar_dir = (cos_theta * cos_phi, cos_theta * sin_phi, -sin_theta * filled)
    azimuth = (-sin_phi * filled, cos_phi * filled, 0.0 * filled)
    return jnp.stack(
        [jnp.stack([radial[axis_at], polar_dir[axis_at], azimuth[axis_at]]) for axis_at in range(3)]
    )


def legendre(colatitude, degrees):
    cosine = jnp.cos(colatitude)[:, None]
    sine = jnp.sin(colatitude)[:, None]
    orders = jnp.arange(degrees, dtype=jnp.float32)[None, :]
    factor = jnp.where(
        orders == 0,
        math.sqrt(0.5),
        -jnp.sqrt((2.0 * orders + 1.0) / jnp.maximum(2.0 * orders, 1.0)) * sine,
    )
    diagonal = jnp.cumprod(factor, axis=1)

    def advance(state_pair, degree):
        previous, before = state_pair
        level = degree.astype(jnp.float32)
        upward = jnp.sqrt(
            jnp.maximum(4.0 * level * level - 1.0, 0.0)
            / jnp.maximum(level * level - orders * orders, 1.0)
        )
        lowered = (level - 1.0) * (level - 1.0)
        downward = jnp.sqrt(
            jnp.maximum(lowered - orders * orders, 0.0) / jnp.maximum(4.0 * lowered - 1.0, 1.0)
        )
        recurred = upward * (cosine * previous - downward * before)
        values = jnp.where(
            orders == level,
            diagonal,
            jnp.where(
                orders + 1.0 == level,
                jnp.sqrt(2.0 * orders + 3.0) * cosine * diagonal,
                jnp.where(orders + 1.0 < level, recurred, 0.0),
            ),
        )
        return ((values, previous), values)

    zeroed = jnp.zeros((colatitude.shape[0], degrees), jnp.float32)
    finals, levels = lax.scan(advance, (zeroed, zeroed), jnp.arange(degrees, dtype=jnp.int32))
    return levels


def doubled(colatitude, degrees):
    levels = legendre(colatitude, degrees)
    return jnp.concatenate((levels, levels), axis=2)


def circle_table(longitude, degrees):
    orders = jnp.arange(degrees, dtype=jnp.float32)[None, :]
    angles = longitude[:, None] * orders
    cosines = jnp.where(
        orders == 0, 1.0 / math.sqrt(2.0 * math.pi), jnp.cos(angles) / math.sqrt(math.pi)
    )
    sines = jnp.where(orders == 0, 0.0, jnp.sin(angles) / math.sqrt(math.pi))
    return jnp.concatenate((cosines, sines), axis=1)


def synthesize(coeffs, circle, levels):
    partial_value = jnp.einsum("ckl,ltc->ktc", coeffs, levels, precision=highest)
    return jnp.einsum("ktc,fc->ktf", partial_value, circle, precision=highest)


def respond(owned_rows, history, kernel):
    stacked = jnp.concatenate((owned_rows[:, None], history), axis=1)
    replies = jnp.einsum("jabl,cjbl->cal", kernel, stacked, precision=highest)
    return (replies, stacked[:, :-1])


def to_grid(values):
    bottom = values[:, :, :, 0, :, :, 0]
    lon_count, lat_count = (bottom.shape[3], bottom.shape[4])
    return bottom.transpose(0, 4, 2, 3, 1).reshape(3, 5 * lat_count, 5 * lon_count)


def from_grid(grid, lon_count, lat_count):
    return grid.reshape(3, lat_count, 5, lon_count, 5).transpose(0, 4, 2, 3, 1)


def on_device(
    displacement,
    velocity,
    rigidity,
    density,
    history,
    kernel,
    owner_order,
    rigid_offset,
    rigid_velocity,
):
    lon_count, lat_count = (displacement.shape[4], displacement.shape[5])
    blk_count, lat_devices = (lax.axis_size(BLK), lax.axis_size(LAT))
    lon_elems, lat_elems = (lon_count * blk_count, lat_count * lat_devices)
    degrees = kernel.shape[3]
    colatitude, longitude, area_weight, face_weight = interface_grid(
        lax.axis_index(LAT) * lat_count,
        lat_count,
        lax.axis_index(BLK) * lon_count,
        lon_count,
        lat_elems,
        lon_elems,
    )
    rotated = rotation(colatitude, longitude)
    levels = doubled(colatitude, degrees)
    circle = circle_table(longitude, degrees)
    inverse = 1.0 / assemble((density * node_volume())[None])
    block_count = 2 * degrees // blk_count
    circle_ordered = jnp.take(circle, owner_order, axis=1)
    block_columns = lax.dynamic_slice_in_dim(
        owner_order, lax.axis_index(BLK) * block_count, block_count, 0
    )
    levels_block = jnp.take(levels, block_columns, axis=2)
    for step_index in range(STEPS):
        relative = to_grid(displacement) - jnp.einsum(
            "jktf,j->ktf", rotated, rigid_offset, precision=highest
        )
        weighted = relative * area_weight
        block_sums = sum_at_owner(
            jnp.einsum("ktf,fc->ckt", weighted, circle_ordered, precision=highest), BLK, 0
        )
        block_partial = jnp.einsum("ckt,ltc->ckl", block_sums, levels_block, precision=highest)
        owned_rows = sum_at_owner(block_partial, LAT, 0)
        replies, history = respond(owned_rows, history, kernel)
        gathered = lax.all_gather(replies, BLK_LAT, axis=0, tiled=True)
        coeffs = jnp.zeros_like(gathered).at[owner_order].set(gathered)
        traction = synthesize(coeffs, circle, levels)
        pull_sum = over_axes(
            jnp.einsum("jktf,ktf->j", rotated * area_weight, traction, precision=highest), BLK_LAT
        )
        rigid_velocity = rigid_velocity + time_step * rigid_gain * pull_sum
        rigid_offset = rigid_offset + time_step * rigid_velocity
        forces = -stiffness(displacement, rigidity)
        forces = forces.at[:, :, :, 0, :, :, 0].add(
            from_grid(-coupling * face_weight * traction, lon_count, lat_count)
        )
        velocity = velocity + time_step * assemble(forces) * inverse
        displacement = displacement + time_step * velocity
    return (displacement, velocity, history, rigid_offset, rigid_velocity)


def solution(mesh):
    split = Mesh(mesh.devices.reshape(4, 8, 2, 2, 2), ("blk_0", "blk_1", "blk_2", "lat_0", "lat_1"))
    in_specs = (
        P(None, None, None, None, BLK, LAT, None),
        P(None, None, None, None, BLK, LAT, None),
        P(None, None, None, BLK, LAT, None),
        P(None, None, None, BLK, LAT, None),
        P(BLK_LAT, None, None, None),
        P(),
        P(),
        P(),
        P(),
    )
    out_specs = (
        P(None, None, None, None, BLK, LAT, None),
        P(None, None, None, None, BLK, LAT, None),
        P(BLK_LAT, None, None, None),
        P(),
        P(),
    )
    return jax.shard_map(
        on_device, mesh=split, in_specs=in_specs, out_specs=out_specs, check_vma=False
    )
```

profile of v0, /device:TPU:1, one launch (start us, length us, event | category | flops | bytes accessed | tf_op | source)
XLA Modules:
  0.0 1690.9 jit_solution(3025484764923406583)
XLA Ops:
  6.8 7.5 collective-permute-start.5
  24.4 6.4 all-to-all-start
  32.6 281.5 %while.46 = (s32[]{:T(128)}, f32[10,128]{1,0:T(8,128)S(1)}, f32[10,128]{1,0:T(8,128)S(1)}, f32[128,10,128]{2,1,0:T(8,128)}, s32[128]{0:T(128)S(1)}, /*index=5*/f...) while((s32[]{:T(128)}, f32[10,128]{1,0:T(8,128)S(1)}, ...), condition=%wide.region_2.3_spmd.clone.clone, body=%wide.region_1.2_spmd.clone.clone.sunk | while | flops 14736 | bytes 38715 | solution.py:216
  325.0 6.2 collective-permute-start.6
  333.3 4.5 collective-permute-done.7
  345.5 347.0 %all_gather.9 = f32[256,3,128]{2,1,0:T(4,128)S(1)} all-gather(f32[1,3,128]{2,1,0:T(4,128)S(1)} %bitcast.584), channel_id=1, replica_groups=mesh['blk_0'=4,'blk_1'=8,'blk_2'=2,'lat_0'=2,'lat_1'=2] {'blk_0','blk_1'..., dimensions={0}, use_global_device_ids=true | all-gather | bytes 394752 | tf_op jit(solution)/shard_map/all_gather | solution.py:300
  692.5 7.0 scatter_fusion
  699.5 3.4 convolution_bitcast_fusion.8
  704.7 6.0 psum.105
  710.9 10.7 psum.106
  721.7 3.8 psum.107
  728.2 5.3 psum.108
  733.5 10.0 psum.109
  744.4 4.1 scatter.101
  748.6 4.1 scatter.104
  752.7 7.1 collective-permute-start.2
  763.1 5.7 collective-permute-done.3
  771.8 5.2 all-to-all-start.2
  778.6 10.0 all-to-all-done.2
  789.6 5.0 all-to-all-start.3
  799.3 341.8 %all_gather.10 = f32[256,3,128]{2,1,0:T(4,128)S(1)} all-gather(f32[1,3,128]{2,1,0:T(4,128)S(1)} %bitcast.585), channel_id=1, replica_groups=mesh['blk_0'=4,'blk_1'=8,'blk_2'=2,'lat_0'=2,'lat_1'=2] {'blk_0','blk_1'..., dimensions={0}, use_global_device_ids=true | all-gather | bytes 394752 | tf_op jit(solution)/shard_map/all_gather | solution.py:300
  1141.2 7.0 scatter_fusion.1
  1148.2 3.4 convolution_bitcast_fusion.7
  1153.6 6.1 psum.110
  1161.6 10.7 psum.111
  1174.9 3.9 psum.112
  1180.3 5.6 psum.113
  1188.1 9.8 psum.114
  1203.5 6.0 collective-permute-done.8
  1209.7 4.0 scatter.124
  1213.7 4.0 scatter.125
  1217.7 5.7 collective-permute-start.10
  1225.5 5.0 collective-permute-done.11
  1234.4 4.8 all-to-all-start.4
  1239.9 11.1 all-to-all-done.4
  1258.9 343.5 %all_gather.11 = f32[256,3,128]{2,1,0:T(4,128)S(1)} all-gather(f32[1,3,128]{2,1,0:T(4,128)S(1)} %bitcast.586), channel_id=1, replica_groups=mesh['blk_0'=4,'blk_1'=8,'blk_2'=2,'lat_0'=2,'lat_1'=2] {'blk_0','blk_1'..., dimensions={0}, use_global_device_ids=true | all-gather | bytes 394752 | tf_op jit(solution)/shard_map/all_gather | solution.py:300
  1602.4 7.0 scatter_fusion.2
  1609.5 3.4 convolution_bitcast_fusion.6
  1614.6 6.1 psum.115
  1621.5 10.7 psum.116
  1634.0 3.8 psum.117
  1638.5 5.4 psum.118
  1644.9 9.8 psum.119
  1660.4 7.0 collective-permute-done.12
  1667.6 4.0 scatter.162
  1671.5 4.0 scatter.163
  1675.6 4.2 collective-permute-start.14
  1681.9 5.0 collective-permute-done.15
  (1499 shorter events, 299.8 us)
Async XLA Ops:
  0.6 30.2 %copy-start.20 = (f32[5,5,1,1,1,1]{1,0,5,4,3,2:T(8,128)S(1)}, f32[5,5,1,1,1,1]{1,0,5,4,3,2:T(8,128)}, u32[]{:S(2)}) copy-start(f32[5,5,1,1,1,1]{1,0,5,4,3,2:T(8,128)} %constant.794) | copy-start | bytes 304
  0.6 30.2 %copy-start = (f32[3,5,5,5,1,2,128]{6,5,4,3,2,1,0:T(2,128)S(1)}, f32[3,5,5,5,1,2,128]{6,5,4,3,2,1,0:T(2,128)}, u32[]{:S(2)}) copy-start(f32[3,5,5,5,1,2,128]{6,5,4,3,2,1,0:T(2,128)} %param.74) | copy-start | bytes 1152004
  4.0 27.4 %copy-start.29 = (f32[1,5,5,5,1,2,128]{6,5,3,2,4,1,0:T(2,128)}, f32[1,5,5,5,1,2,128]{6,5,3,2,4,1,0:T(2,128)S(1)}, u32[]{:S(2)}) copy-start(f32[1,5,5,5,1,2,128]{6,5,3,2,4,1,0:T(2,128)S(1)} %get-tuple-element.628) | copy-start | bytes 384004
  4.7 318.7 %collective-permute-start.4 = (f32[1,5,5,1,2,128]{5,4,2,1,3,0:T(2,128)}, f32[1,5,5,1,2,128]{5,4,2,1,3,0:T(2,128)}, u32[]{:S(2)}, u32[]{:S(2)}) collective-permute-start(f32[1,5,5,1,2,128]{5,4,2,1,3,0:T(2,128)} %get-tuple-element.636), channel_id=1, source_target_pairs={{0,4},{4,8},{8,12},{12,16},{16,20},{20,24},{24,28},{28,32},{32,36}... | collective-permute-start | bytes 76808 | tf_op jit(solution)/shard_map/ppermute | solution.py:31
  6.8 317.3 %collective-permute-start.5 = (f32[1,5,5,1,2,128]{5,4,2,1,3,0:T(2,128)S(1)}, f32[1,5,5,1,2,128]{5,4,2,1,3,0:T(2,128)}, u32[]{:S(2)}, u32[]{:S(2)}) collective-permute-start(f32[1,5,5,1,2,128]{5,4,2,1,3,0:T(2,128)S(1)} %get-tuple-element.635), channel_id=1, source_target_pairs={{4,0},{8,4},{12,8},{16,12},{20,16},{24,20},{28,24},{32,28},{36,32}... | collective-permute-start | bytes 76808 | tf_op jit(solution)/shard_map/ppermute | solution.py:34
  15.0 1126.2 %copy-start.33 = (s32[256]{0:T(256)}, s32[256]{0:T(256)S(1)}, u32[]{:S(2)}) copy-start(s32[256]{0:T(256)S(1)} %compare_select_fusion) | copy-start | bytes 3076
  15.7 754.7 %copy-start.44 = (pred[256]{0:T(512)(128)(4,1)}, pred[256]{0:T(512)(128)(4,1)S(1)}, u32[]{:S(2)}) copy-start(pred[256]{0:T(512)(128)(4,1)S(1)} %compare_and_fusion.1) | copy-start | bytes 772
  24.4 313.8 %all-to-all-start = ((f32[64,4,3,10]{3,1,2,0:T(4,128)}), f32[64,4,3,10]{3,1,2,0:T(4,128)S(1)}, u32[]{:S(2)}, u32[]{:S(2)}) async-start(f32[64,4,3,10]{3,1,2,0:T(4,128)} %copy.581), calls=%async_computation | async-start | bytes 786432 | tf_op jit(solution)/shard_map/all_to_all | solution.py:47
  32.2 756.5 %copy-start.39 = (pred[4]{0:T(512)(128)(4,1)}, pred[4]{0:T(512)(128)(4,1)S(1)}, u32[]{:S(2)}) copy-start(pred[4]{0:T(512)(128)(4,1)S(1)} %get-tuple-element.596) | copy-start | bytes 16
  317.6 861.3 %copy-start.1 = (f32[5,5,5,2,128]{4,0,3,2,1:T(8,128)}, f32[5,5,5,2,128]{4,0,3,2,1:T(8,128)S(1)}, u32[]{:S(2)}) copy-start(f32[5,5,5,2,128]{4,0,3,2,1:T(8,128)S(1)} %copy.561) | copy-start | bytes 384004
  321.1 24.2 %copy-start.23 = (f32[1,63,3,128]{3,1,2,0:T(8,128)}, f32[1,63,3,128]{3,1,2,0:T(8,128)S(1)}, u32[]{:S(2)}) copy-start(f32[1,63,3,128]{3,1,2,0:T(8,128)S(1)} %copy.585) | copy-start | bytes 290308
  321.1 24.3 %copy-start.14 = (f32[64,3,3,128]{3,0,2,1:T(8,128)S(1)}, f32[64,3,3,128]{3,0,2,1:T(8,128)}, u32[]{:S(2)}) copy-start(f32[64,3,3,128]{3,0,2,1:T(8,128)} %param.79) | copy-start | bytes 884740
  325.0 8.2 collective-permute-start.6
  331.3 6.5 collective-permute-start.7
  339.1 6.2 all-to-all-start.1
  702.8 57.0 %copy-start.24 = (f32[1,63,3,128]{3,1,2,0:T(8,128)S(1)}, f32[1,63,3,128]{3,1,2,0:T(8,128)}, u32[]{:S(2)}) copy-start(f32[1,63,3,128]{3,1,2,0:T(8,128)} %copy-done.23) | copy-start | bytes 290308
  725.5 23.0 %collective-permute-start.1 = (f32[3,5,5,1,2,128]{5,4,2,1,0,3:T(2,128)S(1)}, f32[3,5,5,1,2,128]{5,4,2,1,0,3:T(2,128)S(1)}, u32[]{:S(2)}, u32[]{:S(2)}) collective-permute-start(f32[3,5,5,1,2,128]{5,4,2,1,0,3:T(2,128)S(1)} %bitcast.558), channel_id=1, source_target_pairs={{4,0},{8,4},{12,8},{16,12},{20,16},{24,20},{28,24},{32,28},{36,32}... | collective-permute-start | bytes 230408 | tf_op jit(solution)/shard_map/ppermute | solution.py:34
  733.5 10.9 collective-permute-start
  752.7 8.4 collective-permute-start.2
  759.9 39.3 %copy-start.25 = (f32[1,63,3,128]{3,1,2,0:T(8,128)}, f32[1,63,3,128]{3,1,2,0:T(8,128)S(1)}, u32[]{:S(2)}) copy-start(f32[1,63,3,128]{3,1,2,0:T(8,128)S(1)} %fusion.99) | copy-start | bytes 290308
  761.2 7.7 collective-permute-start.3
  771.8 27.5 %copy-start.15 = (f32[64,3,3,128]{3,0,2,1:T(8,128)S(1)}, f32[64,3,3,128]{3,0,2,1:T(8,128)}, u32[]{:S(2)}) copy-start(f32[64,3,3,128]{3,0,2,1:T(8,128)} %param.79) | copy-start | bytes 884740
  771.8 16.8 all-to-all-start.2
  789.6 9.6 all-to-all-start.3
  799.2 349.0 %copy-start.37 = (f32[1,1,3,128]{3,1,2,0:T(1,128)}, f32[1,1,3,128]{3,1,2,0:T(1,128)S(1)}, u32[]{:S(2)}) copy-start(f32[1,1,3,128]{3,1,2,0:T(1,128)S(1)} %broadcast_in_dim.183) | copy-start | bytes 4612
  1153.6 32.3 %copy-start.35 = (f32[5,5,1,1,1,1]{1,0,2,4,5,3:T(8,128)S(1)}, f32[5,5,1,1,1,1]{1,0,2,4,5,3:T(8,128)}, u32[]{:S(2)}) copy-start(f32[5,5,1,1,1,1]{1,0,2,4,5,3:T(8,128)} %constant.795) | copy-start | bytes 304
  1174.9 23.0 %copy-start.49 = (f32[3]{0:T(128)S(1)}, f32[3]{0:T(128)}, u32[]{:S(2)}) copy-start(f32[3]{0:T(128)} %param.82) | copy-start | bytes 40
  1174.9 23.0 %copy-start.51 = (f32[3]{0:T(128)S(1)}, f32[3]{0:T(128)}, u32[]{:S(2)}) copy-start(f32[3]{0:T(128)} %copy-done.50) | copy-start | bytes 40
  1174.9 23.0 %copy-start.42 = (f32[3]{0:T(128)S(1)}, f32[3]{0:T(128)}, u32[]{:S(2)}) copy-start(f32[3]{0:T(128)} %copy-done.41) | copy-start | bytes 40
  1180.3 21.8 %copy-start.26 = (f32[1,63,3,128]{3,1,2,0:T(8,128)S(1)}, f32[1,63,3,128]{3,1,2,0:T(8,128)}, u32[]{:S(2)}) copy-start(f32[1,63,3,128]{3,1,2,0:T(8,128)} %copy-done.25) | copy-start | bytes 290308
  1180.3 21.8 %copy-start.38 = (f32[1,1,3,128]{3,1,2,0:T(1,128)S(1)}, f32[1,1,3,128]{3,1,2,0:T(1,128)}, u32[]{:S(2)}) copy-start(f32[1,1,3,128]{3,1,2,0:T(1,128)} %copy-done.37) | copy-start | bytes 4612
  1199.3 4.1 collective-permute-start.9
  1202.0 7.5 collective-permute-start.8
  1202.1 56.6 %copy-start.21 = (f32[1,63,3,128]{3,1,2,0:T(8,128)}, f32[1,63,3,128]{3,1,2,0:T(8,128)S(1)}, u32[]{:S(2)}) copy-start(f32[1,63,3,128]{3,1,2,0:T(8,128)S(1)} %fusion.97) | copy-start | bytes 290308
  1217.7 7.7 collective-permute-start.10
  1223.4 7.0 collective-permute-start.11
  1234.4 24.5 %copy-start.16 = (f32[64,3,3,128]{3,0,2,1:T(8,128)S(1)}, f32[64,3,3,128]{3,0,2,1:T(8,128)}, u32[]{:S(2)}) copy-start(f32[64,3,3,128]{3,0,2,1:T(8,128)} %param.79) | copy-start | bytes 884740
  1234.4 16.7 all-to-all-start.4
  1239.1 363.3 %copy-start.34 = (s32[256]{0:T(256)S(1)}, s32[256]{0:T(256)}, u32[]{:S(2)}) copy-start(s32[256]{0:T(256)} %copy-done.33) | copy-start | bytes 3076
  1252.0 6.7 all-to-all-start.5
  1614.6 29.3 %copy-start.36 = (f32[5,5,1,1,1,1]{1,0,2,4,5,3:T(8,128)S(1)}, f32[5,5,1,1,1,1]{1,0,2,4,5,3:T(8,128)}, u32[]{:S(2)}) copy-start(f32[5,5,1,1,1,1]{1,0,2,4,5,3:T(8,128)} %constant.795) | copy-start | bytes 304
  1634.0 20.7 %copy-start.43 = (f32[3]{0:T(128)S(1)}, f32[3]{0:T(128)}, u32[]{:S(2)}) copy-start(f32[3]{0:T(128)} %copy-done.41) | copy-start | bytes 40
  1634.0 20.7 %copy-start.47 = (f32[3]{0:T(128)S(1)}, f32[3]{0:T(128)}, u32[]{:S(2)}) copy-start(f32[3]{0:T(128)} %copy-done.46) | copy-start | bytes 40
  1638.5 20.3 %copy-start.22 = (f32[1,63,3,128]{3,1,2,0:T(8,128)S(1)}, f32[1,63,3,128]{3,1,2,0:T(8,128)}, u32[]{:S(2)}) copy-start(f32[1,63,3,128]{3,1,2,0:T(8,128)} %copy-done.21) | copy-start | bytes 290308
  1656.2 4.1 collective-permute-start.13
  1659.6 7.8 collective-permute-start.12
  1675.6 6.2 collective-permute-start.14
  1679.8 7.0 collective-permute-start.15
  (27 other events, 136.0 us)
where the time goes:
time: 1700 us; the launch traced here: 1690 us
  blocking collectives  1140 us (67%)
  local copies, waits for them, and re-layouts  163 us (10%)
  other arithmetic  119 us (7%)
  loops' own time  86.9 us (5%)
  starting transfers between devices  76.8 us (5%)
  waiting for transfers between devices  64.3 us (4%)
  matrix products  38.2 us (2%)
    all_gather x3, blocking collectives, on_device(): gathered = lax.all_gather(replies, BLK_LAT, axis=0, tiled=True)  1030 us
    psum x15, blocking collectives, over_axes(): return functools.reduce(lax.psum, axes, shard)  108 us
    another operation x1, loops' own time, legendre(): lax.scan(advance, (zeroed, zeroed), jnp.arange(degrees, dtype=jnp.int32))  86.9 us
    dynamic_update_slice x128, other arithmetic, legendre(): lax.scan(advance, (zeroed, zeroed), jnp.arange(degrees, dtype=jnp.int32))  86.7 us
    dynamic_slice x128, local copies, waits for them, and re-layouts, legendre(): lax.scan(advance, (zeroed, zeroed), jnp.arange(degrees, dtype=jnp.int32))  82.7 us
  transfers between devices with their start and end apart: 22, of which 14 were waited for; matrix products, arithmetic and copies ran while one was open for 14% of the time, Pallas kernels for 0%

commit v1 on v0

v1 whole, which is shorter than its diff:
```python
import functools
import math

import jax
import jax.numpy as jnp
import numpy as np
from jax import lax
from jax.experimental import pallas as pl
from jax.experimental.pallas import tpu as pltpu
from jax.sharding import Mesh
from jax.sharding import PartitionSpec as P

STEPS = 3
AXES = ("x", "z", "ylo", "yhi", "core")
SIZES = {"x": 4, "z": 8, "ylo": 2, "yhi": 2, "core": 2}
BLK = ("x", "z", "ylo")
LAT = ("yhi", "core")
MESH_ID = pl.DeviceIdType.MESH
FIRST = ("core", "z")
SECOND = ("x", "ylo", "yhi")
GROUP = 16

pole_gap = 0.1
time_step = 0.03
rigid_gain = 20.0
coupling = 1.0


def node_tables():
    points = np.array([-1.0, -math.sqrt(3.0 / 7.0), 0.0, math.sqrt(3.0 / 7.0), 1.0])
    weights = np.array([0.1, 49.0 / 90.0, 32.0 / 45.0, 49.0 / 90.0, 0.1])
    products = np.array(
        [np.prod([points[i] - points[j] for j in range(5) if j != i]) for i in range(5)]
    )
    slopes = np.zeros((5, 5))
    for i in range(5):
        for j in range(5):
            if i == j:
                slopes[i, j] = sum(1.0 / (points[i] - points[o]) for o in range(5) if o != i)
            else:
                slopes[i, j] = products[i] / products[j] / (points[i] - points[j])
    return points, weights, slopes


POINTS, WEIGHTS, SLOPES = node_tables()
THETA_STEP = (math.pi - 2.0 * pole_gap) / 8
PHI_STEP = 2.0 * math.pi / 64
THETA = pole_gap + (np.arange(8)[:, None] + 0.5 * (1.0 + POINTS)) * THETA_STEP
PHI = (np.arange(64)[:, None] + 0.5 * (1.0 + POINTS)) * PHI_STEP


def legendre_table():
    cosine, sine = np.cos(THETA).reshape(-1), np.sin(THETA).reshape(-1)
    table = np.zeros((128, 128, 40))
    diagonal = np.full(40, math.sqrt(0.5))
    for m in range(128):
        if m > 0:
            diagonal = diagonal * -math.sqrt((2 * m + 1) / (2 * m)) * sine
        table[m, m] = diagonal
        if m + 1 < 128:
            table[m, m + 1] = math.sqrt(2 * m + 3) * cosine * diagonal
        for l in range(m + 2, 128):
            up = math.sqrt((4.0 * l * l - 1) / (l * l - m * m))
            low = math.sqrt(((l - 1.0) ** 2 - m * m) / (4.0 * (l - 1.0) ** 2 - 1))
            table[m, l] = up * (cosine * table[m, l - 1] - low * table[m, l - 2])
    padded = np.zeros((128, 8, 8, 128), np.float32)
    padded[:, :, :5] = table.transpose(0, 2, 1).reshape(128, 8, 5, 128)
    return padded.reshape(128, 64, 128)


def circle_values():
    m = np.arange(128)
    angle = m[:, None, None] * PHI[None]
    cosines = np.cos(angle) / math.sqrt(math.pi)
    cosines[0] = 1.0 / math.sqrt(2.0 * math.pi)
    sines = np.sin(angle) / math.sqrt(math.pi)
    sines[0] = 0.0
    return np.concatenate((cosines, sines))


def rotations():
    st, ct = np.sin(THETA)[:, :, None, None], np.cos(THETA)[:, :, None, None]
    sp, cp = np.sin(PHI)[None, None], np.cos(PHI)[None, None]
    one, zero = np.ones((8, 5, 64, 5)), np.zeros((8, 5, 64, 5))
    return np.stack(
        [
            np.stack([st * cp, ct * cp, -sp * one]),
            np.stack([st * sp, ct * sp, cp * one]),
            np.stack([ct * one, -st * one, zero]),
        ]
    )


def areas():
    scale = 0.25 * THETA_STEP * PHI_STEP
    return scale * (WEIGHTS * np.sin(THETA))[:, :, None] * WEIGHTS


def pull_table():
    weighted = np.einsum("yba,jkybea,cea->cjkyb", areas(), rotations(), circle_values())
    table = np.zeros((256, 8, 4, 32))
    for k in range(3):
        for lat in range(4):
            for ey in range(2):
                at = (2 * k + ey) * 5
                table[:, :3, lat, at : at + 5] = weighted[:, :, k, 2 * lat + ey]
    return table.reshape(256, 8, 128).astype(np.float32)


def packed_tables():
    theta_part = np.zeros((4, 3, 8, 128))
    phi_part = np.zeros((64, 2, 8, 128))
    area = areas()
    for r in range(6):
        k, ey = r // 2, r % 2
        for a in range(5):
            for b in range(5):
                lane = 32 * (r % 4) + 5 * a + b
                for lat in range(4):
                    theta = THETA[2 * lat + ey, b]
                    weight = area[2 * lat + ey, b, a]
                    theta_part[lat, 0, r, lane] = weight
                    theta_part[lat, 1, r, lane] = weight * (math.sin(theta), math.cos(theta), 1.0)[k]
                    theta_part[lat, 2, r, lane] = weight * (math.cos(theta), -math.sin(theta), 0.0)[k]
                cp, sp = np.cos(PHI[:, a]), np.sin(PHI[:, a])
                phi_part[:, 0, r, lane] = (cp, cp, -sp)[k]
                phi_part[:, 1, r, lane] = (sp, sp, cp)[k]
    return theta_part.astype(np.float32), phi_part.astype(np.float32)


def circle_at(column, elem, node_shift):
    order = column % 128
    turns = ((order * elem) % 64).astype(jnp.float32) * PHI_STEP
    angle = turns + order.astype(jnp.float32) * node_shift
    cosine = jnp.where(order == 0, 1.0 / math.sqrt(2.0 * math.pi), jnp.cos(angle) / math.sqrt(math.pi))
    sine = jnp.where(order == 0, 0.0, jnp.sin(angle) / math.sqrt(math.pi))
    return jnp.where(column < 128, cosine, sine)


def flat(axes, index):
    at = 0
    for axis in axes:
        at = at * SIZES[axis] + index[axis]
    return at


def unflat(axes, at):
    index = {}
    for axis in reversed(axes):
        index[axis] = at % SIZES[axis]
        at = at // SIZES[axis]
    return index


def partners(axes, me, shifts):
    count = math.prod(SIZES[axis] for axis in axes)
    mine = flat(axes, me)
    found = []
    for shift in shifts:
        other = {**me, **unflat(axes, lax.rem(mine + (shift + count), count))}
        found.append(tuple(other[axis] for axis in AXES))
    return found


def on_sphere(
    u_in, v_in, wr, hist, kern, leg, pull_tab, gt, gs, theta_part, phi_part, x_in, xv_in,
    u, v, hist_out, rigid_out,
    force, inv, gsb, past, coefs, g1, g2, lon_lo, lon_hi, lat_lo, lat_hi,
    send1, recv1, send2, recv2, send_h, recv_h,
):
    me = {axis: lax.axis_index(axis) for axis in AXES}
    lat = flat(LAT, me)
    elem = flat(BLK, me)
    near = partners(FIRST, me, range(1, GROUP))
    far = partners(SECOND, me, range(1, GROUP))
    lon_next, lon_prev = partners(BLK, me, (1, -1))
    lat_next, lat_prev = partners(LAT, me, (1, -1))
    everyone = near + far + [lon_next, lon_prev, lat_next, lat_prev]
    barrier = pltpu.get_barrier_semaphore()
    for other in everyone:
        pl.semaphore_signal(barrier, inc=1, device_id=other, device_id_type=MESH_ID)
    pl.semaphore_wait(barrier, len(everyone))

    lanes = lax.broadcasted_iota(jnp.int32, (8, 128), 1)
    subs = lax.broadcasted_iota(jnp.int32, (8, 128), 0)
    lane_row = lax.broadcasted_iota(jnp.int32, (1, 128), 1)
    even = subs % 2 == 0
    in_field = subs < 6
    slot_near = flat(FIRST, me)
    slot_far = flat(SECOND, me)

    def send(src, dst, ssem, rsem, other):
        copy = pltpu.make_async_remote_copy(
            src_ref=src, dst_ref=dst, send_sem=ssem, recv_sem=rsem,
            device_id=other, device_id_type=MESH_ID,
        )
        copy.start()
        return copy

    def spread(buf, rows, ssem, rsem, step, stage):
        if stage == 0:
            start, count, others = (slot_far * GROUP + slot_near) * rows, rows, near
        else:
            start, count, others = slot_far * GROUP * rows, GROUP * rows, far
        block = buf.at[step, pl.ds(start, count), :]
        return [
            send(block, block, ssem.at[step, stage, d], rsem.at[step, stage, d], other)
            for d, other in enumerate(others)
        ]

    def arrived(copies):
        for copy in copies:
            copy.wait_recv()

    def left(copies):
        for copy in copies:
            copy.wait_send()

    def along(stride, base_of, first):
        def line(i, carry):
            base = base_of(i)
            values = [u[base + q * stride] for q in range(5)]
            weights = [wr[base + q * stride] for q in range(5)]
            grads = []
            for p in range(5):
                total = float(SLOPES[p, 0]) * values[0]
                for q in range(1, 5):
                    total = total + float(SLOPES[p, q]) * values[q]
                grads.append(total * weights[p])
            for q in range(5):
                total = float(SLOPES[0, q]) * grads[0]
                for p in range(1, 5):
                    total = total + float(SLOPES[p, q]) * grads[p]
                at = base + q * stride
                if first:
                    force[at] = jnp.where(in_field, -total, weights[q])
                else:
                    force[at] = force[at] - total
            return carry

        lax.fori_loop(0, 25, line, 0)

    u[...] = u_in[...]
    v[...] = v_in[...]
    coefs[...] = jnp.zeros_like(coefs)

    def prepare():
        for a in range(5):
            gsb[a] = jnp.broadcast_to(gs[:, a : a + 1], (256, 128))
        for step in range(STEPS):
            old = hist[0 : 63 - step]
            for k in range(3):
                rows = jnp.sum(kern[step + 1 : 64, k] * old, axis=0)
                past[step, k : k + 1] = jnp.sum(rows, axis=0, keepdims=True)
        hist_out[3:63] = hist[0:60]

    area = theta_part[lat, 0]
    rig_x = theta_part[lat, 1] * phi_part[elem, 0]
    rig_y = theta_part[lat, 1] * phi_part[elem, 1]
    rig_z = theta_part[lat, 2]

    def one_step(step, state):
        offset, speed = state
        packed = jnp.zeros((8, 128), jnp.float32)
        for i in range(25):
            first_lane = jnp.broadcast_to(u[i * 5][:, 0:1], (8, 128))
            packed = jnp.where(lanes == (subs % 4) * 32 + i, first_lane, packed)
        packed = packed * area - (offset[0] * rig_x + offset[1] * rig_y + offset[2] * rig_z)
        row0 = jnp.sum(packed[0:4], axis=0, keepdims=True)
        row1 = jnp.sum(packed[4:8], axis=0, keepdims=True)
        mine = slot_far * GROUP + slot_near
        g1[step, pl.ds(2 * mine, 2), :] = jnp.concatenate((row0, row1), axis=0)
        copies1 = spread(g1, 2, send1, recv1, step, 0)

        along(25, lambda i: i, True)
        along(5, lambda i: (i // 5) * 25 + i % 5, False)
        along(1, lambda i: i * 5, False)
        for i in range(25):
            low, high = force[i * 5], force[i * 5 + 4]
            force[i * 5] = low + jnp.where(lanes == 0, 0.0, pltpu.roll(high, 1, 1))
            force[i * 5 + 4] = high + jnp.where(lanes == 127, 0.0, pltpu.roll(low, 127, 1))
        up = send(force.at[pl.ds(100, 25)], lon_lo.at[step], send_h.at[step, 0], recv_h.at[step, 0], lon_next)
        down = send(force.at[pl.ds(0, 25)], lon_hi.at[step], send_h.at[step, 1], recv_h.at[step, 1], lon_prev)

        @pl.when(step == 0)
        def _():
            prepare()

        arrived(copies1)
        copies2 = spread(g1, 2, send1, recv1, step, 1)

        up.wait()
        down.wait()
        force[0:25] = force[0:25] + lon_lo[step]
        force[100:125] = force[100:125] + lon_hi[step]
        lat_send = []
        for a in range(5):
            lat_send.append(
                send(force.at[pl.ds(a * 25 + 20, 5)], lat_lo.at[step, pl.ds(a * 5, 5)],
                     send_h.at[step, 2 + a], recv_h.at[step, 2 + a], lat_next)
            )
            lat_send.append(
                send(force.at[pl.ds(a * 25, 5)], lat_hi.at[step, pl.ds(a * 5, 5)],
                     send_h.at[step, 7 + a], recv_h.at[step, 7 + a], lat_prev)
            )

        arrived(copies2)
        field = g1[step].reshape(8, 4, 16, 128)
        summed = jnp.sum(field * gt[...].reshape(8, 1, 16, 128), axis=0)
        summed = summed[:, 0:8] + summed[:, 8:16]
        summed = (summed[:, 0:2] + summed[:, 2:4]) + (summed[:, 4:6] + summed[:, 6:8])
        parts = [jnp.zeros((8, 128), jnp.float32) for k in range(3)]
        for at in range(4):
            for ey in range(2):
                block = leg[(2 * at + ey) * 8 : (2 * at + ey) * 8 + 8]
                for k in range(3):
                    r = 2 * k + ey
                    row = summed[at, r // 4 : r // 4 + 1]
                    local = lanes - 32 * (r % 4)
                    keep = (local >= 0) & (local < 25) & (local % 5 == subs)
                    column = jnp.sum(jnp.where(keep, row, 0.0), axis=1, keepdims=True)
                    parts[k] = parts[k] + column * block
        coef = jnp.concatenate([jnp.sum(part, axis=0, keepdims=True) for part in parts], axis=0)
        coefs[step + 2] = coef
        reply = past[step]
        for k in range(3):
            total = jnp.sum(kern[0, k] * coef, axis=0, keepdims=True)
            for back in (1, 2):
                total = total + jnp.sum(kern[back, k] * coefs[step + 2 - back], axis=0, keepdims=True)
            rep = past[step, k : k + 1] + total
            parts[k] = rep
        message = jnp.zeros((8, 128), jnp.float32)
        for at in range(4):
            for ey in range(2):
                block = leg[(2 * at + ey) * 8 : (2 * at + ey) * 8 + 8]
                for k in range(3):
                    column = jnp.sum(block * parts[k], axis=1, keepdims=True)
                    put = (lanes == 32 * at + (2 * k + ey) * 5 + subs) & (subs < 5)
                    message = jnp.where(put, column, message)
        message = jnp.sum(message, axis=0, keepdims=True)
        pulls = jnp.sum(pull_tab[...] * message, axis=1, keepdims=True)
        for j, lane in enumerate((30, 31, 62)):
            message = message + jnp.where(lane_row == lane, pulls[j : j + 1], 0.0)
        g2[step, pl.ds(mine, 1), :] = message
        copies3 = spread(g2, 1, send2, recv2, step, 0)

        for copy in lat_send:
            copy.wait()
        from_below = jnp.where((subs == 0) & (lat == 0), 0.0, 1.0)
        for a in range(5):
            for c in range(5):
                low, high = force[a * 25 + c], force[a * 25 + 20 + c]
                below, above = lat_lo[step, a * 5 + c], lat_hi[step, a * 5 + c]
                below = jnp.where(lat == 0, 0.0, pltpu.roll(below, 7, 0))
                above = jnp.where(lat == 3, 0.0, pltpu.roll(above, 1, 0))
                force[a * 25 + c] = low + jnp.where(even, below, pltpu.roll(high, 1, 0))
                force[a * 25 + 20 + c] = high + jnp.where(even, pltpu.roll(low, 7, 0), above)

        def advance(i, carry):
            total = force[i]
            inverse = 1.0 / jnp.where(even, total[6:7], total[7:8])
            inv[i] = inverse
            speed_now = v[i] + time_step * (total * inverse)
            speed_now = jnp.where(in_field, speed_now, 0.0)
            v[i] = speed_now
            u[i] = u[i] + time_step * speed_now
            return carry

        lax.fori_loop(0, 125, advance, 0)

        arrived(copies3)
        copies4 = spread(g2, 1, send2, recv2, step, 1)
        left(copies1)
        left(copies2)
        arrived(copies4)

        field = g2[step]
        whole = jnp.sum(field, axis=0, keepdims=True)
        new_offset, new_speed = [], []
        for j, lane in enumerate((30, 31, 62)):
            pull = jnp.sum(jnp.where(lane_row == lane, whole, 0.0), axis=1, keepdims=True)
            new_speed.append(speed[j] + time_step * rigid_gain * pull)
            new_offset.append(offset[j] + time_step * new_speed[j])
        edge = lanes == 0
        for a in range(5):
            row = jnp.sum(field * gsb[a], axis=0, keepdims=True)
            along_lon = float(WEIGHTS[a] * (2.0 if a in (0, 4) else 1.0))
            for b in range(5):
                local = lanes - 32 * lat
                here = (local == subs * 5 + b) & in_field
                traction = jnp.sum(jnp.where(here, row, 0.0), axis=1, keepdims=True)
                face = float(coupling * WEIGHTS[b]) * along_lon
                if b == 0:
                    face = face * jnp.where(even & (lat == 0), 1.0, 2.0)
                if b == 4:
                    face = face * jnp.where((~even) & (lat == 3), 1.0, 2.0)
                i = (a * 5 + b) * 5
                gain = jnp.where(edge, time_step * (traction * face) * inv[i], 0.0)
                v[i] = v[i] - gain
                u[i] = u[i] - time_step * gain
        left(copies3)
        left(copies4)
        return tuple(new_offset), tuple(new_speed)

    start = (
        tuple(jnp.full((1, 1), x_in[j], jnp.float32) for j in range(3)),
        tuple(jnp.full((1, 1), xv_in[j], jnp.float32) for j in range(3)),
    )
    offset, speed = lax.fori_loop(0, STEPS, one_step, start)
    for step in range(STEPS):
        hist_out[step] = coefs[STEPS + 1 - step]
    for j in range(3):
        rigid_out[j : j + 1] = jnp.broadcast_to(offset[j], (1, 128))
        rigid_out[3 + j : 4 + j] = jnp.broadcast_to(speed[j], (1, 128))


def to_rows(field):
    return field.transpose(1, 2, 3, 0, 4, 5, 6).reshape(125, -1, 128)


def from_rows(rows):
    return rows[:, :6].reshape(5, 5, 5, 3, 1, 2, 128).transpose(3, 0, 1, 2, 4, 5, 6)


def on_device(
    displacement, velocity, rigidity, density, history, kernel, owner_order, rigid_offset, rigid_velocity
):
    elem = lax.axis_index(BLK)
    column = lax.dynamic_index_in_dim(owner_order, lax.axis_index(AXES), 0, keepdims=False)
    legendre = lax.dynamic_index_in_dim(jnp.asarray(legendre_table()), column % 128, 0, keepdims=False)
    pull_tab = lax.dynamic_index_in_dim(jnp.asarray(pull_table()), column, 0, keepdims=False)
    shift = jnp.asarray(0.5 * (1.0 + POINTS) * PHI_STEP, dtype=jnp.float32)
    row = np.arange(128)
    x, ylo, z = row // 32, row // 16 % 2, row // 2 % 8
    lane = np.arange(128) % 32
    lane_shift = 0.5 * (1.0 + POINTS[np.minimum(lane // 5, 4)]) * PHI_STEP
    row_elem = jnp.asarray(((x * 8 + z) * 2 + ylo)[:, None], dtype=jnp.int32)
    own_circle = circle_at(column, row_elem, jnp.asarray(lane_shift[None], dtype=jnp.float32))
    own_circle = jnp.where(jnp.asarray(lane[None] < 25), own_circle, 0.0)
    slots = owner_order.reshape(4, 8, 2, 2, 2).transpose(0, 2, 3, 4, 1).reshape(256, 1)
    lane_circle = circle_at(slots, elem, jnp.pad(shift, (0, 3))[None])
    theta_part, phi_part = packed_tables()

    u8 = jnp.pad(to_rows(displacement), ((0, 0), (0, 2), (0, 0)))
    v8 = jnp.pad(to_rows(velocity), ((0, 0), (0, 2), (0, 0)))
    volume = (WEIGHTS[:, None, None] * WEIGHTS[:, None] * WEIGHTS).reshape(125, 1, 1).astype(np.float32)
    rig2, den2 = rigidity.reshape(125, 2, 128), density.reshape(125, 2, 128)
    wr = jnp.concatenate((rig2, rig2, rig2, den2), axis=1) * volume

    vmem = pl.BlockSpec(memory_space=pltpu.VMEM)
    smem = pl.BlockSpec(memory_space=pltpu.SMEM)
    sds = functools.partial(jax.ShapeDtypeStruct, dtype=jnp.float32)
    new_u, new_v, new_history, rigid = pl.pallas_call(
        on_sphere,
        out_shape=(sds((125, 8, 128)), sds((125, 8, 128)), sds((63, 3, 128)), sds((8, 128))),
        in_specs=[vmem] * 11 + [smem] * 2,
        out_specs=(vmem,) * 4,
        scratch_shapes=[
            pltpu.VMEM((125, 8, 128), jnp.float32),
            pltpu.VMEM((125, 8, 128), jnp.float32),
            pltpu.VMEM((5, 256, 128), jnp.float32),
            pltpu.VMEM((STEPS, 8, 128), jnp.float32),
            pltpu.VMEM((STEPS + 2, 3, 128), jnp.float32),
            pltpu.VMEM((STEPS, 512, 128), jnp.float32),
            pltpu.VMEM((STEPS, 256, 128), jnp.float32),
            pltpu.VMEM((STEPS, 25, 8, 128), jnp.float32),
            pltpu.VMEM((STEPS, 25, 8, 128), jnp.float32),
            pltpu.VMEM((STEPS, 25, 8, 128), jnp.float32),
            pltpu.VMEM((STEPS, 25, 8, 128), jnp.float32),
            pltpu.SemaphoreType.DMA((STEPS, 2, GROUP - 1)),
            pltpu.SemaphoreType.DMA((STEPS, 2, GROUP - 1)),
            pltpu.SemaphoreType.DMA((STEPS, 2, GROUP - 1)),
            pltpu.SemaphoreType.DMA((STEPS, 2, GROUP - 1)),
            pltpu.SemaphoreType.DMA((STEPS, 12)),
            pltpu.SemaphoreType.DMA((STEPS, 12)),
        ],
        compiler_params=pltpu.CompilerParams(
            collective_id=0, has_side_effects=True, vmem_limit_bytes=40 * 1024 * 1024
        ),
    )(
        u8, v8, wr, history[0], kernel, legendre, pull_tab, own_circle, lane_circle,
        jnp.asarray(theta_part), jnp.asarray(phi_part), rigid_offset, rigid_velocity,
    )
    return from_rows(new_u), from_rows(new_v), new_history[None], rigid[0:3, 0], rigid[3:6, 0]


def solution(mesh):
    split = Mesh(mesh.devices.reshape(4, 8, 2, 2, 2), AXES)
    field = P(None, None, None, None, BLK, LAT, None)
    scalar_field = P(None, None, None, BLK, LAT, None)
    owned = P(AXES, None, None, None)
    return jax.shard_map(
        on_device,
        mesh=split,
        in_specs=(field, field, scalar_field, scalar_field, owned, P(), P(), P(), P()),
        out_specs=(field, field, owned, P(), P()),
        check_vma=False,
    )
```

time: 1700 us -> 103 us (0.06)
  blocking collectives: 1140 us -> 0 us
  local copies, waits for them, and re-layouts: 163 us -> 11.6 us
  other arithmetic: 119 us -> 3.79 us
  loops' own time: 86.9 us -> 0 us
  Pallas kernels: 0 us -> 82.1 us
  starting transfers between devices: 76.8 us -> 0 us
  waiting for transfers between devices: 64.3 us -> 0 us
  matrix products: 38.2 us -> 0 us
    all_gather x3 -> x0, blocking collectives: 1030 us -> none  [on_device(): gathered = lax.all_gather(replies, BLK_LAT, axis=0, tiled=True)]
    psum x15 -> x0, blocking collectives: 108 us -> none  [over_axes(): return functools.reduce(lax.psum, axes, shard)]
    another operation x1 -> x0, loops' own time: 86.9 us -> none  [legendre(): lax.scan(advance, (zeroed, zeroed), jnp.arange(degrees, dtype=jnp.int32))]
    dynamic_update_slice x128 -> x0, other arithmetic: 86.7 us -> none  [legendre(): lax.scan(advance, (zeroed, zeroed), jnp.arange(degrees, dtype=jnp.int32))]
    pallas_call x0 -> x1, Pallas kernels: none -> 82.1 us  [on_device(): pl.pallas_call(on_sphere, out_shape=(sds((125, 8, 128)), sds((125, 8, 128...]
    dynamic_slice x128 -> x1, local copies, waits for them, and re-layouts: 82.7 us -> 1.34 us  [on_device(): lax.dynamic_index_in_dim(owner_order, lax.axis_index(AXES), 0, keepdims=F...]
    ppermute x16 -> x0, starting transfers between devices: 49 us -> none  [the longest x8 25.8 us: with_halo(): lax.ppermute(lax.slice_in_dim(block, block.shape[dim] - width, None, axis...]
    scatter x14 -> x0, local copies, waits for them, and re-layouts: 45.1 us -> none  [the longest x6 24.1 us: assemble(): forces = forces.at[:, 0].set(lower).at[:, 4].set(upper)]
  transfers between devices with their start and end apart: 22 -> 0, of which waited for: 14 -> 0; matrix products, arithmetic and copies ran while one was open for 14% -> 0% of each run, Pallas kernels for 0% -> 0%
where the time goes in v1:
time: 103 us; the launch traced here: 102 us
  Pallas kernels  82.1 us (80%)
  local copies, waits for them, and re-layouts  11.6 us (11%)
  between operations  4.8 us (5%)
  other arithmetic  3.79 us (4%)
    pallas_call x1, Pallas kernels, on_device(): pl.pallas_call(on_sphere, out_shape=(sds((125, 8, 128)), sds((125, 8, 128...  82.1 us
    unnamed x21, local copies, waits for them, and re-layouts  3.64 us
    transpose x2, local copies, waits for them, and re-layouts, to_rows(): return field.transpose(1, 2, 3, 0, 4, 5, 6).reshape(125, -1, 128)  2.25 us

profile of v1, /device:TPU:1, one launch (start us, length us, event | category | flops | bytes accessed | tf_op | source)
XLA Modules:
  0.0 102.3 jit_solution(8319667507219446765)
XLA Ops:
  0.6 0.0 copy-start.7
  0.6 0.0 copy-start
  0.7 0.0 copy-start.1
  0.7 0.0 copy-start.3
  0.7 0.0 copy-start.2
  0.7 0.0 copy-start.4
  0.7 0.0 copy-start.5
  0.7 0.0 copy-start.6
  0.7 1.3 %dynamic_slice.12 = s32[1]{0:T(128)} dynamic-slice(s32[256]{0:T(256)} %param.24, s32[]{:T(128)S(6)} %select_n.88), dynamic_slice_sizes={1} | dynamic-slice | bytes 12 | tf_op jit(solution)/shard_map/jit(dynamic_index_in_dim)/dynamic_slice | solution.py:429
  6.0 0.7 multiply_bitcast_fusion
  6.6 0.7 fusion.13
  7.3 0.7 dynamic-slice_bitcast_fusion.1.pull_tab
  8.0 0.8 dynamic-slice_bitcast_fusion.leg
  8.8 1.0 fusion.3.gt
  9.7 0.8 reshape.115
  10.6 0.2 copy.32
  10.8 0.1 reshape.116
  10.9 0.9 copy.39
  11.8 0.1 copy.33.hist
  11.9 1.2 %select_select_fusion.gs = f32[256,8]{1,0:T(8,128)S(1)} fusion(f32[8]{0:T(128)} %constant.140, f32[256]{0:T(256)S(1)} %convert_element_type.30, f32[256]{0:T(256)S(1)} %fusion.7, pred[256]{0:T(512)(128)(4,1)S(1)} %get-tuple-element.25, pred[256]{0:T(512)(128)(4,1)S(1)} %get-tuple-element.27), kind=kLoop, calls=%fused_computation.1 | loop fusion | flops 14336 | bytes 10784 | tf_op jit(solution)/shard_map/jit(_where)/select_n | solution.py:137
  13.1 1.1 %copy.29 = f32[5,5,5,3,1,2,128]{6,5,3,2,1,0,4:T(2,128)S(1)} copy(f32[5,5,5,3,1,2,128]{6,5,4,2,1,0,3:T(2,128)} %bitcast.32) | data formatting | bytes 768000 | tf_op jit(solution)/shard_map/transpose | solution.py:418
  14.3 0.3 reshape.111
  14.6 1.1 %copy.30 = f32[5,5,5,3,1,2,128]{6,5,3,2,1,0,4:T(2,128)S(1)} copy(f32[5,5,5,3,1,2,128]{6,5,4,2,1,0,3:T(2,128)} %bitcast.33) | data formatting | bytes 768000 | tf_op jit(solution)/shard_map/transpose | solution.py:418
  15.7 0.3 reshape.112
  16.0 0.0 copy-done.4
  16.0 0.2 copy.34.kern
  16.2 0.0 copy-done.7
  16.3 0.0 copy-done.5
  16.3 0.0 copy-done.6
  16.3 0.2 maximum_multiply_fusion.wr
  16.5 0.0 copy-done
  16.5 0.0 copy-done.1
  16.5 0.0 copy-done.3
  16.5 0.0 copy-done.2
  16.5 82.1 %shard_map.209 = (f32[125,8,128]{2,1,0:T(8,128)S(1)}, f32[125,8,128]{2,1,0:T(8,128)S(1)}, f32[63,3,128]{2,1,0:T(4,128)S(1)}, f32[8,128]{1,0:T(8,128)S(1)}) custom-call(f32[125,8,128]{2,1,0:T(8,128)S(1)} %pad.11.u_in, f32[125,8,128]{2,1,0:T(8,128)S(1)} %pad.12.v_in, f32[125,8,128]{2,1,0:T(8,128)S(1)} %maximum_multiply_fusion.wr, ...), custom_call_target="tpu_custom_call" | custom-call | tf_op jit(solution)/shard_map/pallas_call | solution.py:453
  98.7 0.2 reshape.117
  98.9 0.9 copy.35
  99.8 0.2 reshape.118
  100.0 0.9 copy.36
  100.9 0.7 slice_reduce_fusion
  101.5 0.7 copy.37
  (5 shorter events, 0.1 us)
Async XLA Ops:
  0.6 15.6 %copy-start.7 = (f32[125]{0:T(128)S(1)}, f32[125]{0:T(128)}, u32[]{:S(2)}) copy-start(f32[125]{0:T(128)} %constant.138) | copy-start | bytes 1504
  0.6 15.9 %copy-start = (f32[64,2,8,128]{3,2,1,0:T(8,128)S(1)}, f32[64,2,8,128]{3,2,1,0:T(8,128)}, u32[]{:S(2)}) copy-start(f32[64,2,8,128]{3,2,1,0:T(8,128)} %constant.126.clone.phi_part) | copy-start | bytes 1572868
  0.7 15.9 %copy-start.1 = (f32[4,3,8,128]{3,2,1,0:T(8,128)S(1)}, f32[4,3,8,128]{3,2,1,0:T(8,128)}, u32[]{:S(2)}) copy-start(f32[4,3,8,128]{3,2,1,0:T(8,128)} %constant.125.clone.theta_part) | copy-start | bytes 147460
  0.7 15.9 %copy-start.3 = (f32[3]{0:T(128)S(1)}, f32[3]{0:T(128)}, u32[]{:S(2)}) copy-start(f32[3]{0:T(128)} %xv_in.1) | copy-start | bytes 40
  0.7 15.9 %copy-start.2 = (f32[3]{0:T(128)S(1)}, f32[3]{0:T(128)}, u32[]{:S(2)}) copy-start(f32[3]{0:T(128)} %x_in.1) | copy-start | bytes 40
  0.7 15.3 %copy-start.4 = (f32[64,3,3,128]{3,0,2,1:T(8,128)S(1)}, f32[64,3,3,128]{3,0,2,1:T(8,128)}, u32[]{:S(2)}) copy-start(f32[64,3,3,128]{3,0,2,1:T(8,128)} %param.23) | copy-start | bytes 884740
  0.7 15.6 %copy-start.5 = (f32[5,5,5,1,2,128]{5,4,3,2,1,0:T(2,128)S(1)}, f32[5,5,5,1,2,128]{5,4,3,2,1,0:T(2,128)}, u32[]{:S(2)}) copy-start(f32[5,5,5,1,2,128]{5,4,3,2,1,0:T(2,128)} %param.21) | copy-start | bytes 384004
  0.7 15.6 %copy-start.6 = (f32[5,5,5,1,2,128]{5,4,3,2,1,0:T(2,128)S(1)}, f32[5,5,5,1,2,128]{5,4,3,2,1,0:T(2,128)}, u32[]{:S(2)}) copy-start(f32[5,5,5,1,2,128]{5,4,3,2,1,0:T(2,128)} %param.20) | copy-start | bytes 384004

commit v2 on v1

v2 whole, which is shorter than its diff:
```python
import functools
import math

import jax
import jax.numpy as jnp
import numpy as np
from jax import lax
from jax.experimental import pallas as pl
from jax.experimental.pallas import tpu as pltpu
from jax.sharding import Mesh
from jax.sharding import PartitionSpec as P

STEPS = 3
AXES = ("x", "z", "ylo", "yhi", "core")
SIZES = {"x": 4, "z": 8, "ylo": 2, "yhi": 2, "core": 2}
BLK = ("x", "z", "ylo")
LAT = ("yhi", "core")
MESH_ID = pl.DeviceIdType.MESH
FIRST = ("core", "z")
SECOND = ("x", "ylo", "yhi")
GROUP = 16
PLANE = ("x", "ylo", "yhi", "core")

pole_gap = 0.1
time_step = 0.03
rigid_gain = 20.0
coupling = 1.0


def node_tables():
    points = np.array([-1.0, -math.sqrt(3.0 / 7.0), 0.0, math.sqrt(3.0 / 7.0), 1.0])
    weights = np.array([0.1, 49.0 / 90.0, 32.0 / 45.0, 49.0 / 90.0, 0.1])
    products = np.array(
        [np.prod([points[i] - points[j] for j in range(5) if j != i]) for i in range(5)]
    )
    slopes = np.zeros((5, 5))
    for i in range(5):
        for j in range(5):
            if i == j:
                slopes[i, j] = sum(1.0 / (points[i] - points[o]) for o in range(5) if o != i)
            else:
                slopes[i, j] = products[i] / products[j] / (points[i] - points[j])
    return points, weights, slopes


POINTS, WEIGHTS, SLOPES = node_tables()
THETA_STEP = (math.pi - 2.0 * pole_gap) / 8
PHI_STEP = 2.0 * math.pi / 64
THETA = pole_gap + (np.arange(8)[:, None] + 0.5 * (1.0 + POINTS)) * THETA_STEP
PHI = (np.arange(64)[:, None] + 0.5 * (1.0 + POINTS)) * PHI_STEP


def legendre_table():
    cosine, sine = np.cos(THETA).reshape(-1), np.sin(THETA).reshape(-1)
    table = np.zeros((128, 128, 40))
    diagonal = np.full(40, math.sqrt(0.5))
    for m in range(128):
        if m > 0:
            diagonal = diagonal * -math.sqrt((2 * m + 1) / (2 * m)) * sine
        table[m, m] = diagonal
        if m + 1 < 128:
            table[m, m + 1] = math.sqrt(2 * m + 3) * cosine * diagonal
        for l in range(m + 2, 128):
            up = math.sqrt((4.0 * l * l - 1) / (l * l - m * m))
            low = math.sqrt(((l - 1.0) ** 2 - m * m) / (4.0 * (l - 1.0) ** 2 - 1))
            table[m, l] = up * (cosine * table[m, l - 1] - low * table[m, l - 2])
    return table.transpose(0, 2, 1).astype(np.float32)


def circle_values():
    m = np.arange(128)
    angle = m[:, None, None] * PHI[None]
    cosines = np.cos(angle) / math.sqrt(math.pi)
    cosines[0] = 1.0 / math.sqrt(2.0 * math.pi)
    sines = np.sin(angle) / math.sqrt(math.pi)
    sines[0] = 0.0
    return np.concatenate((cosines, sines))


def rotations():
    st, ct = np.sin(THETA)[:, :, None, None], np.cos(THETA)[:, :, None, None]
    sp, cp = np.sin(PHI)[None, None], np.cos(PHI)[None, None]
    one, zero = np.ones((8, 5, 64, 5)), np.zeros((8, 5, 64, 5))
    return np.stack(
        [
            np.stack([st * cp, ct * cp, -sp * one]),
            np.stack([st * sp, ct * sp, cp * one]),
            np.stack([ct * one, -st * one, zero]),
        ]
    )


def areas():
    scale = 0.25 * THETA_STEP * PHI_STEP
    return scale * (WEIGHTS * np.sin(THETA))[:, :, None] * WEIGHTS


def pull_table():
    weighted = np.einsum("yba,jkybea,cea->cjkyb", areas(), rotations(), circle_values())
    table = np.zeros((256, 8, 4, 32))
    for k in range(3):
        for lat in range(4):
            for ey in range(2):
                at = (2 * k + ey) * 5
                table[:, :3, lat, at : at + 5] = weighted[:, :, k, 2 * lat + ey]
    return table.reshape(256, 8, 128).astype(np.float32)


def packed_tables():
    table = np.zeros((4, 3, 8, 128))
    area = areas()
    for lat in range(4):
        for r in range(6):
            for a in range(5):
                for b in range(5):
                    ey = r % 2
                    weight = area[2 * lat + ey, b, a]
                    table[lat, a // 4, r, 32 * (a % 4) + 5 * r + b] = weight
                    if r < 2:
                        copies = 2.0 if a in (0, 4) else 1.0
                        pole = (lat, ey, b) in ((0, 0, 0), (3, 1, 4))
                        copies *= 2.0 if b in (0, 4) and not pole else 1.0
                        face = coupling * WEIGHTS[a] * WEIGHTS[b] * copies
                        table[lat, 2, r, 32 + 10 * a + 5 * ey + b] = time_step**2 * weight * face
    return table.astype(np.float32)


def column_tables():
    table = np.zeros((256, 16, 128))
    e = np.arange(64)
    elem = ((e // 16) * 8 + e % 8) * 2 + e // 8 % 2
    m = np.arange(128)
    turn = m[:, None] * elem * PHI_STEP
    shift = m[:, None] * (0.5 * (1.0 + POINTS) * PHI_STEP)
    scale = np.full((128, 1), 1.0 / math.sqrt(math.pi))
    scale[0] = 1.0 / math.sqrt(2.0 * math.pi)
    real = np.ones((128, 1))
    real[0] = 0.0
    for kind in range(2):
        cols = slice(128 * kind, 128 * kind + 128)
        for pair in range(2):
            table[cols, 2 * pair, pair::2] = np.cos(turn)
            table[cols, 2 * pair + 1, pair::2] = np.sin(turn)
            for a in range(4) if pair == 0 else (4,):
                lanes = slice(32 * (a % 4), 32 * (a % 4) + 30)
                if kind == 0:
                    first, second = scale[:, 0] * np.cos(shift[:, a]), -scale[:, 0] * np.sin(shift[:, a])
                else:
                    first, second = (real * scale)[:, 0] * np.sin(shift[:, a]), (real * scale)[:, 0] * np.cos(shift[:, a])
                table[cols, 4 + 2 * pair, lanes] = first[:, None]
                table[cols, 5 + 2 * pair, lanes] = second[:, None]
    table[:, 8:11] = pull_table()[:, :3]
    circle = np.zeros((256, 384))
    circle[:, :320] = circle_values()[:, elem].transpose(0, 2, 1).reshape(256, 320)
    table[:, 11:14] = circle.reshape(256, 3, 128)
    return table.astype(np.float32)


def flat(axes, index):
    at = 0
    for axis in axes:
        at = at * SIZES[axis] + index[axis]
    return at


def unflat(axes, at):
    index = {}
    for axis in reversed(axes):
        index[axis] = at % SIZES[axis]
        at = at // SIZES[axis]
    return index


def partners(axes, me, shifts):
    count = math.prod(SIZES[axis] for axis in axes)
    mine = flat(axes, me)
    found = []
    for shift in shifts:
        other = {**me, **unflat(axes, lax.rem(mine + (shift + count), count))}
        found.append(tuple(other[axis] for axis in AXES))
    return found


def on_sphere(
    u_in, v_in, rig_in, den_in, volume, hist, kern, leg_in, cols_in, packing, order, x_in, xv_in,
    u_out, v_out, hist_out, rigid_out,
    u, v, wr, force, inv, face_force, leg, cols, lp, e32, d32, q8, gown, gtt, ga, gsb, wi, past, coefs, g1, g2,
    lon_lo, lon_hi, lat_lo, lat_hi,
    load_sem, store_sem, send1, recv1, send2, recv2, send_p, recv_p, send_h, recv_h,
):
    me = {axis: lax.axis_index(axis) for axis in AXES}
    lat, depth = flat(LAT, me), me["z"]
    near = partners(FIRST, me, range(1, GROUP))
    far = partners(SECOND, me, range(1, GROUP))
    plane = partners(PLANE, me, range(1, 32))
    column_mates = partners(("z",), me, range(1, 8))
    lon_next, lon_prev = partners(BLK, me, (1, -1))
    lat_next, lat_prev = partners(LAT, me, (1, -1))
    everyone = near + plane + [lon_next, lon_prev, lat_next, lat_prev]
    barrier = pltpu.get_barrier_semaphore()
    for other in everyone:
        pl.semaphore_signal(barrier, inc=1, device_id=other, device_id_type=MESH_ID)

    u[...] = jnp.zeros_like(u)
    v[...] = jnp.zeros_like(v)
    loads = []

    def load(src, dst):
        copy = pltpu.make_async_copy(src, dst, load_sem.at[len(loads)])
        copy.start()
        loads.append(copy)

    for k in range(3):
        load(u_in.at[k], u.at[:, pl.ds(2 * k, 2), :])
    for k in range(3):
        load(rig_in, wr.at[:, pl.ds(2 * k, 2), :])
    load(den_in, wr.at[:, pl.ds(6, 2), :])
    for k in range(3):
        load(v_in.at[k], v.at[:, pl.ds(2 * k, 2), :])
    load(cols_in, cols)
    load(leg_in, leg)

    lanes = lax.broadcasted_iota(jnp.int32, (8, 128), 1)
    subs = lax.broadcasted_iota(jnp.int32, (8, 128), 0)
    slant = lanes - 5 * subs
    even = subs % 2 == 0
    in_field = subs < 6
    slot_near, slot_far, slot_plane = flat(FIRST, me), flat(SECOND, me), flat(PLANE, me)
    mine = slot_far * GROUP + slot_near

    def send(src, dst, ssem, rsem, other):
        copy = pltpu.make_async_remote_copy(
            src_ref=src, dst_ref=dst, send_sem=ssem, recv_sem=rsem,
            device_id=other, device_id_type=MESH_ID,
        )
        copy.start()
        return copy

    def spread(at, stage):
        if stage == 0:
            start, count, others = mine * 2, 2, near
        else:
            start, count, others = slot_far * GROUP * 2, GROUP * 2, far
        block = g1.at[at, pl.ds(start, count), :]
        return [
            send(block, block, send1.at[at, stage, d], recv1.at[at, stage, d], other)
            for d, other in enumerate(others)
        ]

    def arrived(copies):
        for copy in copies:
            copy.wait_recv()

    unsent = []

    def copies_of(a, b):
        count = 2.0 if a in (0, 4) else 1.0
        if b == 0:
            return count * jnp.where(even & (lat == 0), 1.0, 2.0)
        if b == 4:
            return count * jnp.where((~even) & (lat == 3), 1.0, 2.0)
        return count

    def pack(value, first=None):
        packed = [jnp.zeros((8, 128), jnp.float32) for row in range(2)]
        for a in range(5):
            for b in range(5):
                node = jnp.broadcast_to(value(a, b)[:, 0:1], (8, 128))
                if first is None:
                    row, at = a // 4, 32 * (a % 4) + b
                else:
                    row, at = 0, first + 10 * a + b
                packed[row] = jnp.where(slant == at, node, packed[row])
        return packed

    def post(at, value, tail=None):
        packed = pack(value)
        rows = [packed[row] * packing[lat, row] for row in range(2)]
        if tail is not None:
            rows[1] = rows[1] + tail
        g1[at, pl.ds(2 * mine, 2), :] = jnp.concatenate(
            [jnp.sum(row, axis=0, keepdims=True) for row in rows], axis=0
        )
        copies = spread(at, 0)
        unsent.extend(copies)
        return copies

    def forward(at):
        copies = spread(at, 1)
        unsent.extend(copies)
        return copies

    def gradients(base, stride):
        values = [u[base + q * stride] for q in range(5)]
        weights = [wr[base + q * stride] for q in range(5)]
        grads = []
        for p in range(5):
            total = float(SLOPES[p, 0]) * values[0]
            for q in range(1, 5):
                total = total + float(SLOPES[p, q]) * values[q]
            grads.append(total * weights[p])
        return grads, weights

    def divergence(grads, q):
        total = float(SLOPES[0, q]) * grads[0]
        for p in range(1, 5):
            total = total + float(SLOPES[p, q]) * grads[p]
        return total

    def along(stride, base_of, first):
        def line(i, carry):
            base = base_of(i)
            grads, weights = gradients(base, stride)
            for q in range(5):
                total = divergence(grads, q)
                at = base + q * stride
                if first:
                    force[at] = jnp.where(in_field, -total, weights[q])
                else:
                    force[at] = force[at] - total
            return carry

        lax.fori_loop(0, 25, line, 0)

    def stiffness():
        along(25, lambda i: i, True)
        along(5, lambda i: (i // 5) * 25 + i % 5, False)
        along(1, lambda i: i * 5, False)

    def interface_stiffness():
        def radial(i, carry):
            grads, weights = gradients(i * 5, 1)
            face_force[i] = -divergence(grads, 0)
            return carry

        def flat_lines(i, carry):
            grads, weights = gradients(i * 5, 25)
            for q in range(5):
                face_force[q * 5 + i] = face_force[q * 5 + i] - divergence(grads, q)
            grads, weights = gradients(i * 25, 5)
            for q in range(5):
                face_force[i * 5 + q] = face_force[i * 5 + q] - divergence(grads, q)
            return carry

        lax.fori_loop(0, 25, radial, 0)
        lax.fori_loop(0, 5, flat_lines, 0)

    def join_radial():
        for i in range(25):
            low, high = force[i * 5], force[i * 5 + 4]
            force[i * 5] = low + jnp.where(lanes == 0, 0.0, pltpu.roll(high, 1, 1))
            force[i * 5 + 4] = high + jnp.where(lanes == 127, 0.0, pltpu.roll(low, 127, 1))

    def lon_out(step):
        return [
            send(force.at[pl.ds(100, 25)], lon_lo.at[step], send_h.at[step, 0], recv_h.at[step, 0], lon_next),
            send(force.at[pl.ds(0, 25)], lon_hi.at[step], send_h.at[step, 1], recv_h.at[step, 1], lon_prev),
        ]

    def lon_in_lat_out(step, copies):
        for copy in copies:
            copy.wait()
        force[0:25] = force[0:25] + lon_lo[step]
        force[100:125] = force[100:125] + lon_hi[step]
        out = []
        for a in range(5):
            out.append(
                send(force.at[pl.ds(a * 25 + 20, 5)], lat_lo.at[step, pl.ds(a * 5, 5)],
                     send_h.at[step, 2 + a], recv_h.at[step, 2 + a], lat_next)
            )
            out.append(
                send(force.at[pl.ds(a * 25, 5)], lat_hi.at[step, pl.ds(a * 5, 5)],
                     send_h.at[step, 7 + a], recv_h.at[step, 7 + a], lat_prev)
            )
        return out

    def lat_in(step, copies):
        for copy in copies:
            copy.wait()
        for a in range(5):
            for c in range(5):
                low, high = force[a * 25 + c], force[a * 25 + 20 + c]
                below, above = lat_lo[step, a * 5 + c], lat_hi[step, a * 5 + c]
                below = jnp.where(lat == 0, 0.0, pltpu.roll(below, 7, 0))
                above = jnp.where(lat == 3, 0.0, pltpu.roll(above, 1, 0))
                force[a * 25 + c] = low + jnp.where(even, below, pltpu.roll(high, 1, 0))
                force[a * 25 + 20 + c] = high + jnp.where(even, pltpu.roll(low, 7, 0), above)

    def advance():
        def node(i, carry):
            speed_now = jnp.where(in_field, v[i] + time_step * (force[i] * inv[i]), 0.0)
            v[i] = speed_now
            u[i] = u[i] + time_step * speed_now
            return carry

        lax.fori_loop(0, 125, node, 0)

    def predicted(a, b):
        i = a * 5 + b
        push = (time_step**2 * copies_of(a, b)) * (inv[i * 5] * face_force[i])
        return u[i * 5] + time_step * v[i * 5] + push

    def analysed(at):
        field = g1[at].reshape(8, 4, 16, 128)
        field = jnp.concatenate([field[:, i].reshape(128, 128) for i in range(4)], axis=1)
        sums = jnp.dot(e32[...], field, precision=lax.Precision.HIGHEST, preferred_element_type=jnp.float32)
        result = jnp.zeros((8, 128), jnp.float32)
        for i in range(4):
            part = d32[0:8] * sums[0:8, 128 * i : 128 * i + 128]
            for q in range(1, 4):
                part = part + d32[8 * q : 8 * q + 8] * sums[8 * q : 8 * q + 8, 128 * i : 128 * i + 128]
            part = part + pltpu.roll(part, 64, 1)
            part = part + pltpu.roll(part, 32, 1)
            result = jnp.where(lanes // 32 == i, part, result)
        return result

    def owners(step, sums, offset):
        for j in range(3):
            sums = sums - offset[j] * q8[j]
        found = [jnp.zeros((8, 128), jnp.float32) for k in range(3)]
        for t in range(40):
            block = lp[t]
            for k in range(3):
                lane = (t // 10) * 32 + (2 * k + t // 5 % 2) * 5 + t % 5
                found[k] = found[k] + sums[:, lane : lane + 1] * block
        replies = []
        for k in range(3):
            coefs[step + 2, k] = found[k]
            row = jnp.sum(jnp.where(subs == depth, found[k], 0.0), axis=0, keepdims=True)
            hist_out[STEPS - 1 - step, k : k + 1] = row
        for k in range(3):
            reply = past[3 * step + k]
            for i in range(3):
                reply = reply + kern[0, k, i : i + 1] * found[i]
                for back in range(1, step + 1):
                    reply = reply + kern[back, k, i : i + 1] * coefs[step + 2 - back, i]
            replies.append(reply)
        message = jnp.zeros((8, 128), jnp.float32)
        for t in range(40):
            block = lp[t]
            for k in range(3):
                lane = (t // 10) * 32 + (2 * k + t // 5 % 2) * 5 + t % 5
                value = jnp.sum(block * replies[k], axis=1, keepdims=True)
                message = jnp.where(lanes == lane, value, message)
        pulls = [jnp.sum(message * q8[j], axis=1, keepdims=True) for j in range(3)]
        for j, lane in enumerate((30, 31, 62)):
            message = jnp.where(lanes == lane, pulls[j], message)
        block = g2.at[step, pl.ds(8 * slot_plane, 8), :]
        g2[step, pl.ds(8 * slot_plane, 8), :] = message
        copies = [send(block, block, send2.at[step, d], recv2.at[step, d], other) for d, other in enumerate(plane)]
        unsent.extend(copies)
        return copies

    def rigid_step(step, offset, speed):
        whole = jnp.sum(g2[step], axis=0, keepdims=True)
        lane_row = lax.broadcasted_iota(jnp.int32, (1, 128), 1)
        new_offset, new_speed = [], []
        for j, lane in enumerate((30, 31, 62)):
            pull = jnp.sum(jnp.where(lane_row == lane, whole, 0.0), axis=1, keepdims=True)
            new_speed.append(speed[j] + time_step * rigid_gain * pull)
            new_offset.append(offset[j] + time_step * new_speed[j])
        return new_offset, new_speed

    def add_traction(step):
        field = g2[step]
        edge = lanes == 0
        for a in range(5):
            row = jnp.sum(field * gsb[a], axis=0, keepdims=True)
            for b in range(5):
                here = (slant == 32 * lat + b) & in_field
                traction = jnp.sum(jnp.where(here, row, 0.0), axis=1, keepdims=True)
                face = float(coupling * WEIGHTS[a] * WEIGHTS[b]) * copies_of(a, b)
                i = (a * 5 + b) * 5
                gain = jnp.where(edge, time_step * (traction * face) * inv[i], 0.0)
                v[i] = v[i] - gain
                u[i] = u[i] - time_step * gain

    def moved(step):
        total = jnp.zeros((8, 128), jnp.float32)
        for q, (start, count) in enumerate(((0, 128), (128, 128), (256, 64))):
            traction = jnp.dot(
                ga[start : start + count], g2[step], precision=lax.Precision.HIGHEST,
                preferred_element_type=jnp.float32,
            )
            total = total + jnp.dot(
                gown[q, :, 0:count], traction * wi[start : start + count], precision=lax.Precision.HIGHEST,
                preferred_element_type=jnp.float32,
            )
        return total

    def mine_of(position):
        return order[position]

    for copy in loads[0:3]:
        copy.wait()
    packed_start = pack(lambda a, b: u[(a * 5 + b) * 5])
    pl.semaphore_wait(barrier, len(everyone))
    rows = [packed_start[row] * packing[lat, row] for row in range(2)]
    g1[0, pl.ds(2 * mine, 2), :] = jnp.concatenate([jnp.sum(row, axis=0, keepdims=True) for row in rows], axis=0)
    wave0 = spread(0, 0)
    unsent.extend(wave0)

    for step in range(STEPS):
        old = hist[0 : 63 - step]
        for k in range(3):
            total = jnp.sum(kern[step + 1 : 64, k] * old, axis=0)
            past[3 * step + k, pl.ds(depth, 1), :] = jnp.sum(total, axis=0, keepdims=True)
    own_past = past.at[:, pl.ds(depth, 1), :]
    wave_past = [
        send(own_past, own_past, send_p.at[d], recv_p.at[d], other) for d, other in enumerate(column_mates)
    ]
    unsent.extend(wave_past)

    for copy in loads[3:10]:
        copy.wait()

    def weigh(i, carry):
        wr[i] = wr[i] * volume[i]
        return carry

    lax.fori_loop(0, 125, weigh, 0)
    stiffness()
    for i in range(25):
        face_force[i] = force[i * 5]
    join_radial()
    lon = lon_out(0)

    for copy in loads[10:]:
        copy.wait()
    base = (me["x"] * 16 + me["ylo"]) * 4 + lat
    own = [order[base + 8 * i] for i in range(8)]
    for i in range(8):
        for q in range(4):
            e32[8 * q + i : 8 * q + i + 1] = cols[own[i], q : q + 1]
            d32[8 * q + i : 8 * q + i + 1] = cols[own[i], 4 + q : 5 + q]
        for q in range(3):
            q8[q, i : i + 1] = cols[own[i], 8 + q : 9 + q]
            gown[q, i : i + 1] = cols[own[i], 11 + q : 12 + q]

    def take(t, carry):
        for i in range(8):
            lp[t, i : i + 1] = leg[lax.rem(own[i], 128), pl.ds(t, 1), :]
        return carry

    lax.fori_loop(0, 40, take, 0)
    arrived(wave0)
    wave0 = forward(0)

    lat_copies = lon_in_lat_out(0, lon)

    def circle_row(s, carry):
        i, rest = s % 8, s // 8
        column = order[((rest // 8) * 16 + i * 2 + rest // 4 % 2) * 4 + rest % 4]
        for q in range(3):
            gtt[q, pl.ds(s, 1), :] = cols[column, 11 + q : 12 + q]
        return carry

    lax.fori_loop(0, 256, circle_row, 0)
    many = lax.broadcasted_iota(jnp.int32, (256, 128), 1)
    elem = (me["x"] * 2 + me["ylo"]) * 8 + depth
    for a in range(5):
        picked = jnp.where(many == elem + 64 * (a % 2), gtt[a // 2], 0.0)
        gsb[a] = jnp.broadcast_to(jnp.sum(picked, axis=1, keepdims=True), (256, 128))
    for q in range(3):
        ga[128 * q : 128 * q + 128] = jnp.transpose(gtt[q])
    hist_out[3:63] = hist[0:60]
    arrived(wave_past)

    offset = [jnp.full((1, 1), x_in[j], jnp.float32) for j in range(3)]
    speed = [jnp.full((1, 1), xv_in[j], jnp.float32) for j in range(3)]

    arrived(wave0)
    replies0 = owners(0, analysed(0), offset)
    lat_in(0, lat_copies)

    def invert(i, carry):
        mass = force[i]
        inv[i] = 1.0 / jnp.where(even, mass[6:7], mass[7:8])
        return carry

    lax.fori_loop(0, 125, invert, 0)
    tail = pack(lambda a, b: inv[(a * 5 + b) * 5], 32)[0] * packing[lat, 2]
    wave1 = post(1, predicted, tail)
    advance()
    arrived(wave1)
    wave1 = forward(1)
    arrived(replies0)
    add_traction(0)
    offset, speed = rigid_step(0, offset, speed)

    interface_stiffness()
    wave2 = post(2, predicted)
    stiffness()
    join_radial()
    lon = lon_out(1)
    arrived(wave1)
    factors = g1[1, pl.ds(1, 256, 2), :].reshape(8, 4, 8, 128)
    wide = lax.broadcasted_iota(jnp.int32, (64, 128), 1)
    for a in range(5):
        total = jnp.zeros((64, 128), jnp.float32)
        for i in range(4):
            block = factors[:, i].reshape(64, 128)
            for k in range(3):
                start = 32 * i + 10 * k
                turned = pltpu.roll(block, (start - 32 - 10 * a) % 128, 1)
                total = jnp.where((wide >= start) & (wide < start + 10), turned, total)
        wi[64 * a : 64 * a + 64] = total
    replies1 = owners(1, analysed(1) - moved(0), offset)
    arrived(wave2)
    wave2 = forward(2)
    lat_copies = lon_in_lat_out(1, lon)
    lat_in(1, lat_copies)
    advance()
    arrived(replies1)
    add_traction(1)
    offset, speed = rigid_step(1, offset, speed)

    stiffness()
    join_radial()
    lon = lon_out(2)
    shift = moved(1)
    arrived(wave2)
    replies2 = owners(2, analysed(2) - shift, offset)
    lat_copies = lon_in_lat_out(2, lon)
    lat_in(2, lat_copies)
    advance()
    arrived(replies2)
    add_traction(2)
    offset, speed = rigid_step(2, offset, speed)

    stores = []
    for k in range(3):
        for n, (src, dst) in enumerate(((u, u_out), (v, v_out))):
            copy = pltpu.make_async_copy(src.at[:, pl.ds(2 * k, 2), :], dst.at[k], store_sem.at[2 * k + n])
            copy.start()
            stores.append(copy)
    for j in range(3):
        rigid_out[j : j + 1] = jnp.broadcast_to(offset[j], (1, 128))
        rigid_out[3 + j : 4 + j] = jnp.broadcast_to(speed[j], (1, 128))
    rigid_out[6:8] = jnp.zeros((2, 128), jnp.float32)
    for copy in unsent:
        copy.wait_send()
    for copy in stores:
        copy.wait()


def on_device(
    displacement, velocity, rigidity, density, history, kernel, owner_order, rigid_offset, rigid_velocity
):
    volume = (WEIGHTS[:, None, None] * WEIGHTS[:, None] * WEIGHTS).reshape(125).astype(np.float32)
    vmem = pl.BlockSpec(memory_space=pltpu.VMEM)
    smem = pl.BlockSpec(memory_space=pltpu.SMEM)
    hbm = pl.BlockSpec(memory_space=pl.ANY)
    sds = functools.partial(jax.ShapeDtypeStruct, dtype=jnp.float32)
    state = (125, 8, 128)
    sem = pltpu.SemaphoreType.DMA
    new_u, new_v, new_history, rigid = pl.pallas_call(
        on_sphere,
        out_shape=(sds((3, 125, 2, 128)), sds((3, 125, 2, 128)), sds((63, 3, 128)), sds((8, 128))),
        in_specs=[hbm] * 4 + [smem, vmem, vmem, hbm, hbm, vmem] + [smem] * 3,
        out_specs=(hbm, hbm, vmem, vmem),
        scratch_shapes=[
            pltpu.VMEM(shape, jnp.float32)
            for shape in (
                state, state, state, state, state, (25, 8, 128),
                (128, 40, 128), (256, 16, 128), (40, 8, 128), (32, 128), (32, 128), (3, 8, 128), (3, 8, 128),
                (3, 256, 128), (384, 256), (5, 256, 128), (320, 128), (9, 8, 128), (STEPS + 2, 3, 8, 128),
                (STEPS, 512, 128), (STEPS, 256, 128),
            )
            + ((STEPS, 25, 8, 128),) * 4
        ]
        + [
            sem((12,)), sem((6,)), sem((STEPS, 2, GROUP - 1)), sem((STEPS, 2, GROUP - 1)),
            sem((STEPS, 31)), sem((STEPS, 31)), sem((7,)), sem((7,)), sem((STEPS, 12)), sem((STEPS, 12)),
        ],
        compiler_params=pltpu.CompilerParams(
            collective_id=0, has_side_effects=True, vmem_limit_bytes=40 * 1024 * 1024
        ),
    )(
        displacement.reshape(3, 125, 2, 128), velocity.reshape(3, 125, 2, 128),
        rigidity.reshape(125, 2, 128), density.reshape(125, 2, 128), jnp.asarray(volume),
        history[0], kernel, jnp.asarray(legendre_table()), jnp.asarray(column_tables()),
        jnp.asarray(packed_tables()), owner_order, rigid_offset, rigid_velocity,
    )
    shape = displacement.shape
    return new_u.reshape(shape), new_v.reshape(shape), new_history[None], rigid[0:3, 0], rigid[3:6, 0]


def solution(mesh):
    split = Mesh(mesh.devices.reshape(4, 8, 2, 2, 2), AXES)
    field = P(None, None, None, None, BLK, LAT, None)
    scalar_field = P(None, None, None, BLK, LAT, None)
    owned = P(AXES, None, None, None)
    return jax.shard_map(
        on_device,
        mesh=split,
        in_specs=(field, field, scalar_field, scalar_field, owned, P(), P(), P(), P()),
        out_specs=(field, field, owned, P(), P()),
        check_vma=False,
    )
```

time: 103 us -> 94.4 us (0.917)
  Pallas kernels: 82.1 us -> 77.8 us
  between operations: 4.8 us -> 0.67 us
  local copies, waits for them, and re-layouts: 11.6 us -> 15.6 us
  other arithmetic: 3.79 us -> 0 us
    unnamed x21 -> x27, local copies, waits for them, and re-layouts: 3.64 us -> 14.9 us
    pallas_call x1, Pallas kernels: 82.1 us -> 77.8 us  [on_device(): pl.pallas_call(on_sphere, out_shape=(sds((3, 125, 2, 128)), sds((3, 125,...]
    transpose x3 -> x0, local copies, waits for them, and re-layouts: 2.42 us -> none  [the longest x2 2.25 us: to_rows(): return field.transpose(1, 2, 3, 0, 4, 5, 6).reshape(125, -1, 128)]
    select_n x2 -> x0, other arithmetic: 2.2 us -> none  [the longest x1 1.23 us: circle_at(): return jnp.where(column < 128, cosine, sine)]
    reshape x6 -> x0, local copies, waits for them, and re-layouts: 1.92 us -> none  [the longest x2 0.95 us: on_device(): owner_order.reshape(4, 8, 2, 2, 2).transpose(0, 2, 3, 4, 1).reshape(256, 1)]
    squeeze x2 -> x0, local copies, waits for them, and re-layouts: 1.45 us -> none  [the longest x1 0.76 us: on_device(): lax.dynamic_index_in_dim(jnp.asarray(legendre_table()), column % 128, 0,...]
    dynamic_slice x1 -> x0, local copies, waits for them, and re-layouts: 1.34 us -> none  [on_device(): lax.dynamic_index_in_dim(owner_order, lax.axis_index(AXES), 0, keepdims=F...]
    add x2 -> x0, other arithmetic: 1.33 us -> none  [circle_at(): angle = turns + order.astype(jnp.float32) * node_shift]
where the time goes in v2:
time: 94.4 us; the launch traced here: 94 us
  Pallas kernels  77.8 us (82%)
  local copies, waits for them, and re-layouts  15.6 us (17%)
    pallas_call x1, Pallas kernels, on_device(): pl.pallas_call(on_sphere, out_shape=(sds((3, 125, 2, 128)), sds((3, 125,...  77.8 us
    unnamed x27, local copies, waits for them, and re-layouts  14.9 us

profile of v2, /device:TPU:1, one launch (start us, length us, event | category | flops | bytes accessed | tf_op | source)
XLA Modules:
  0.0 94.0 jit_solution(7962003215769833820)
XLA Ops:
  0.6 0.9 copy.29
  1.5 0.1 copy.23.hist
  1.6 1.2 %copy.24.kern = f32[64,3,3,128]{3,2,1,0:T(4,128)S(1)} copy(f32[64,3,3,128]{3,0,2,1:T(8,128)} %param.18) | data formatting | bytes 589824 | tf_op args[5]
  2.8 0.0 copy-start
  2.8 1.7 %copy-done = f32[128,40,128]{2,1,0:T(8,128)S(1)} copy-done((f32[128,40,128]{2,1,0:T(8,128)S(1)}, f32[128,40,128]{2,1,0:T(8,128)}, u32[]{:S(2)}) %copy-start) | copy-done | bytes 2621464
  4.5 0.0 copy-start.1
  4.5 1.6 %copy-done.1 = f32[256,16,128]{2,1,0:T(8,128)S(1)} copy-done((f32[256,16,128]{2,1,0:T(8,128)S(1)}, f32[256,16,128]{2,1,0:T(8,128)}, u32[]{:S(2)}) %copy-start.1) | copy-done | bytes 2097176
  6.1 0.0 copy-start.2
  6.1 1.0 %copy-done.2 = f32[3,5,5,5,1,2,128]{6,5,4,3,2,1,0:T(2,128)S(1)} copy-done((f32[3,5,5,5,1,2,128]{6,5,4,3,2,1,0:T(2,128)S(1)}, f32[3,5,5,5,1,2,128]{6,5,4,3,2,1,0:T(2,128)}, u32[]{:S(2)}) %copy-start.2) | copy-done | bytes 384024
  7.1 0.0 copy-start.3
  7.1 1.0 %copy-done.3 = f32[3,5,5,5,1,2,128]{6,5,4,3,2,1,0:T(2,128)S(1)} copy-done((f32[3,5,5,5,1,2,128]{6,5,4,3,2,1,0:T(2,128)S(1)}, f32[3,5,5,5,1,2,128]{6,5,4,3,2,1,0:T(2,128)}, u32[]{:S(2)}) %copy-start.3) | copy-done | bytes 384024
  8.1 0.0 copy-start.4
  8.1 0.9 copy-done.4
  9.0 0.0 copy-start.5
  9.0 0.9 copy-done.5
  9.9 0.0 copy-start.6
  9.9 0.8 copy-done.6
  10.7 0.0 copy-start.7
  10.7 0.7 copy-done.7
  11.4 0.0 copy-start.8
  11.4 0.7 copy-done.8
  12.0 0.0 copy-start.9
  12.0 0.7 copy-done.9
  12.7 0.0 copy-start.10
  12.7 0.7 copy-done.10
  13.4 77.8 %shard_map.164 = (f32[3,125,2,128]{3,2,1,0:T(2,128)S(1)}, f32[3,125,2,128]{3,2,1,0:T(2,128)S(1)}, f32[63,3,128]{2,1,0:T(4,128)S(1)}, f32[8,128]{1,0:T(8,128)S(1)}) custom-call(f32[3,125,2,128]{3,2,1,0:T(2,128)S(1)} %bitcast.14, f32[3,125,2,128]{3,2,1,0:T(2,128)S(1)} %bitcast.15, f32[125,2,128]{2,1,0:T(2,128)S(1)} %bitcast.19, f32[125,2,128]{2,1,0:T(2,128)S(1)} %bitcast.20, ...), custom_call_target="tpu_custom_call" | custom-call | tf_op jit(solution)/shard_map/pallas_call | solution.py:657
  91.1 0.7 slice_reduce_fusion
  91.8 0.7 copy.27
  92.5 0.7 copy.32
  93.3 0.7 copy.33
Async XLA Ops:
  2.8 1.7 %copy-start = (f32[128,40,128]{2,1,0:T(8,128)S(1)}, f32[128,40,128]{2,1,0:T(8,128)}, u32[]{:S(2)}) copy-start(f32[128,40,128]{2,1,0:T(8,128)} %constant.9.clone.leg_in) | copy-start | bytes 7864324
  4.5 1.6 %copy-start.1 = (f32[256,16,128]{2,1,0:T(8,128)S(1)}, f32[256,16,128]{2,1,0:T(8,128)}, u32[]{:S(2)}) copy-start(f32[256,16,128]{2,1,0:T(8,128)} %constant.10.clone.cols_in) | copy-start | bytes 6291460
  6.1 1.0 %copy-start.2 = (f32[3,5,5,5,1,2,128]{6,5,4,3,2,1,0:T(2,128)S(1)}, f32[3,5,5,5,1,2,128]{6,5,4,3,2,1,0:T(2,128)}, u32[]{:S(2)}) copy-start(f32[3,5,5,5,1,2,128]{6,5,4,3,2,1,0:T(2,128)} %param.13) | copy-start | bytes 1152004
  7.1 1.0 %copy-start.3 = (f32[3,5,5,5,1,2,128]{6,5,4,3,2,1,0:T(2,128)S(1)}, f32[3,5,5,5,1,2,128]{6,5,4,3,2,1,0:T(2,128)}, u32[]{:S(2)}) copy-start(f32[3,5,5,5,1,2,128]{6,5,4,3,2,1,0:T(2,128)} %param.14) | copy-start | bytes 1152004
  8.1 0.9 copy-start.4
  9.0 0.9 copy-start.5
  9.9 0.8 copy-start.6
  10.7 0.7 copy-start.7
  11.4 0.7 copy-start.8
  12.0 0.7 copy-start.9
  12.7 0.7 copy-start.10

commit v3 on v2

--- a/solution.py
+++ b/solution.py
@@ -11,6 +11,7 @@
 from jax.sharding import PartitionSpec as P
 
 STEPS = 3
+VMEM_BYTES = 60 * 1024 * 1024
 AXES = ("x", "z", "ylo", "yhi", "core")
 SIZES = {"x": 4, "z": 8, "ylo": 2, "yhi": 2, "core": 2}
 BLK = ("x", "z", "ylo")
@@ -182,10 +183,10 @@
 
 
 def on_sphere(
-    u_in, v_in, rig_in, den_in, volume, hist, kern, leg_in, cols_in, packing, order, x_in, xv_in,
+    u_in, v_in, rig_in, den_in, volume, hist_in, kern, leg_in, cols_in, packing, order, x_in, xv_in,
     u_out, v_out, hist_out, rigid_out,
-    u, v, wr, force, inv, face_force, leg, cols, lp, e32, d32, q8, gown, gtt, ga, gsb, wi, past, coefs, g1, g2,
-    lon_lo, lon_hi, lat_lo, lat_hi,
+    un, vn, rn, dn, u, v, wr, force, inv, face_force, hist, leg, cols, lp, e32, d32, q8, gown, gtt, ga, gsb, wi, past, coefs, g1, g2,
+    lon_lo, lon_hi, lat_lo, lat_hi, edges,
     load_sem, store_sem, send1, recv1, send2, recv2, send_p, recv_p, send_h, recv_h,
 ):
     me = {axis: lax.axis_index(axis) for axis in AXES}
@@ -196,13 +197,12 @@
     column_mates = partners(("z",), me, range(1, 8))
     lon_next, lon_prev = partners(BLK, me, (1, -1))
     lat_next, lat_prev = partners(LAT, me, (1, -1))
-    everyone = near + plane + [lon_next, lon_prev, lat_next, lat_prev]
+    corners = [lon[:3] + colat[3:] for lon in (lon_next, lon_prev) for colat in (lat_next, lat_prev)]
+    everyone = near + plane + [lon_next, lon_prev, lat_next, lat_prev] + corners
     barrier = pltpu.get_barrier_semaphore()
     for other in everyone:
         pl.semaphore_signal(barrier, inc=1, device_id=other, device_id_type=MESH_ID)
 
-    u[...] = jnp.zeros_like(u)
-    v[...] = jnp.zeros_like(v)
     loads = []
 
     def load(src, dst):
@@ -210,13 +210,12 @@
         copy.start()
         loads.append(copy)
 
-    for k in range(3):
-        load(u_in.at[k], u.at[:, pl.ds(2 * k, 2), :])
-    for k in range(3):
-        load(rig_in, wr.at[:, pl.ds(2 * k, 2), :])
-    load(den_in, wr.at[:, pl.ds(6, 2), :])
-    for k in range(3):
-        load(v_in.at[k], v.at[:, pl.ds(2 * k, 2), :])
+    load(u_in, un)
+    load(rig_in, rn)
+    load(den_in, dn)
+    load(v_in, vn)
+    hist[0:16] = jnp.zeros((16, 128), jnp.float32)
+    load(hist_in.at[:, 0, :], hist.at[pl.ds(9, 189), :])
     load(cols_in, cols)
     load(leg_in, leg)
 
@@ -351,49 +350,69 @@
             force[i * 5] = low + jnp.where(lanes == 0, 0.0, pltpu.roll(high, 1, 1))
             force[i * 5 + 4] = high + jnp.where(lanes == 127, 0.0, pltpu.roll(low, 127, 1))
 
-    def lon_out(step):
+    def halo_out(step):
+        moves = [
+            (pl.ds(100, 25), lon_lo.at[step], lon_next),
+            (pl.ds(0, 25), lon_hi.at[step], lon_prev),
+            (pl.ds(120, 5), edges.at[step, 0], corners[0]),
+            (pl.ds(100, 5), edges.at[step, 1], corners[1]),
+            (pl.ds(20, 5), edges.at[step, 2], corners[2]),
+            (pl.ds(0, 5), edges.at[step, 3], corners[3]),
+        ]
+        for a in range(5):
+            moves.append((pl.ds(25 * a + 20, 5), lat_lo.at[step, pl.ds(5 * a, 5)], lat_next))
+            moves.append((pl.ds(25 * a, 5), lat_hi.at[step, pl.ds(5 * a, 5)], lat_prev))
         return [
-            send(force.at[pl.ds(100, 25)], lon_lo.at[step], send_h.at[step, 0], recv_h.at[step, 0], lon_next),
-            send(force.at[pl.ds(0, 25)], lon_hi.at[step], send_h.at[step, 1], recv_h.at[step, 1], lon_prev),
+            send(force.at[rows], dst, send_h.at[step, n], recv_h.at[step, n], other)
+            for n, (rows, dst, other) in enumerate(moves)
         ]
 
-    def lon_in_lat_out(step, copies):
+    def halo_in(step, copies):
         for copy in copies:
             copy.wait()
         force[0:25] = force[0:25] + lon_lo[step]
         force[100:125] = force[100:125] + lon_hi[step]
-        out = []
-        for a in range(5):
-            out.append(
-                send(force.at[pl.ds(a * 25 + 20, 5)], lat_lo.at[step, pl.ds(a * 5, 5)],
-                     send_h.at[step, 2 + a], recv_h.at[step, 2 + a], lat_next)
-            )
-            out.append(
-                send(force.at[pl.ds(a * 25, 5)], lat_hi.at[step, pl.ds(a * 5, 5)],
-                     send_h.at[step, 7 + a], recv_h.at[step, 7 + a], lat_prev)
-            )
-        return out
-
-    def lat_in(step, copies):
-        for copy in copies:
-            copy.wait()
         for a in range(5):
             for c in range(5):
                 low, high = force[a * 25 + c], force[a * 25 + 20 + c]
                 below, above = lat_lo[step, a * 5 + c], lat_hi[step, a * 5 + c]
+                if a == 0:
+                    below, above = below + edges[step, 0, c], above + edges[step, 1, c]
+                if a == 4:
+                    below, above = below + edges[step, 2, c], above + edges[step, 3, c]
                 below = jnp.where(lat == 0, 0.0, pltpu.roll(below, 7, 0))
                 above = jnp.where(lat == 3, 0.0, pltpu.roll(above, 1, 0))
                 force[a * 25 + c] = low + jnp.where(even, below, pltpu.roll(high, 1, 0))
                 force[a * 25 + 20 + c] = high + jnp.where(even, pltpu.roll(low, 7, 0), above)
 
-    def advance():
-        def node(i, carry):
-            speed_now = jnp.where(in_field, v[i] + time_step * (force[i] * inv[i]), 0.0)
-            v[i] = speed_now
-            u[i] = u[i] + time_step * speed_now
+    def node_step(i):
+        speed_now = jnp.where(in_field, v[i] + time_step * (force[i] * inv[i]), 0.0)
+        v[i] = speed_now
+        u[i] = u[i] + time_step * speed_now
+
+    def inside(body):
+        def line(t, carry):
+            for c in range(5):
+                body(25 * (1 + t // 3) + 5 * (1 + t % 3) + c)
             return carry
 
-        lax.fori_loop(0, 125, node, 0)
+        lax.fori_loop(0, 9, line, 0)
+
+    def around(body):
+        def ends(t, carry):
+            for c in range(5):
+                body(5 * t + c)
+                body(100 + 5 * t + c)
+            return carry
+
+        def middle(t, carry):
+            for c in range(5):
+                body(25 * t + c)
+                body(25 * t + 20 + c)
+            return carry
+
+        lax.fori_loop(0, 5, ends, 0)
+        lax.fori_loop(1, 4, middle, 0)
 
     def predicted(a, b):
         i = a * 5 + b
@@ -427,13 +446,13 @@
         for k in range(3):
             coefs[step + 2, k] = found[k]
             row = jnp.sum(jnp.where(subs == depth, found[k], 0.0), axis=0, keepdims=True)
-            hist_out[STEPS - 1 - step, k : k + 1] = row
+            hist[3 * (STEPS - 1 - step) + k : 3 * (STEPS - 1 - step) + k + 1] = row
         for k in range(3):
             reply = past[3 * step + k]
             for i in range(3):
-                reply = reply + kern[0, k, i : i + 1] * found[i]
+                reply = reply + kern[k, i, 0:1] * found[i]
                 for back in range(1, step + 1):
-                    reply = reply + kern[back, k, i : i + 1] * coefs[step + 2 - back, i]
+                    reply = reply + kern[k, i, back : back + 1] * coefs[step + 2 - back, i]
             replies.append(reply)
         message = jnp.zeros((8, 128), jnp.float32)
         for t in range(40):
@@ -461,7 +480,7 @@
             new_offset.append(offset[j] + time_step * new_speed[j])
         return new_offset, new_speed
 
-    def add_traction(step):
+    def add_traction(step, shared_moved=True):
         field = g2[step]
         edge = lanes == 0
         for a in range(5):
@@ -473,7 +492,8 @@
                 i = (a * 5 + b) * 5
                 gain = jnp.where(edge, time_step * (traction * face) * inv[i], 0.0)
                 v[i] = v[i] - gain
-                u[i] = u[i] - time_step * gain
+                if shared_moved or (0 < a < 4 and 0 < b < 4):
+                    u[i] = u[i] - time_step * gain
 
     def moved(step):
         total = jnp.zeros((8, 128), jnp.float32)
@@ -488,45 +508,43 @@
             )
         return total
 
-    def mine_of(position):
-        return order[position]
+    none = jnp.zeros((2, 128), jnp.float32)
+
+    def stacked(field, i):
+        return jnp.concatenate([field[0, i], field[1, i], field[2, i], none], axis=0)
+
+    def by_fives(body):
+        def five(t, carry):
+            for i in range(5):
+                body(5 * t + i)
+            return carry
+
+        lax.fori_loop(0, 25, five, 0)
 
     for copy in loads[0:3]:
         copy.wait()
+
+    def stack_state(i):
+        u[i] = stacked(un, i)
+        wr[i] = jnp.concatenate([rn[i], rn[i], rn[i], dn[i]], axis=0) * volume[i]
+
+    by_fives(stack_state)
     packed_start = pack(lambda a, b: u[(a * 5 + b) * 5])
-    pl.semaphore_wait(barrier, len(everyone))
     rows = [packed_start[row] * packing[lat, row] for row in range(2)]
     g1[0, pl.ds(2 * mine, 2), :] = jnp.concatenate([jnp.sum(row, axis=0, keepdims=True) for row in rows], axis=0)
-    wave0 = spread(0, 0)
-    unsent.extend(wave0)
-
-    for step in range(STEPS):
-        old = hist[0 : 63 - step]
-        for k in range(3):
-            total = jnp.sum(kern[step + 1 : 64, k] * old, axis=0)
-            past[3 * step + k, pl.ds(depth, 1), :] = jnp.sum(total, axis=0, keepdims=True)
-    own_past = past.at[:, pl.ds(depth, 1), :]
-    wave_past = [
-        send(own_past, own_past, send_p.at[d], recv_p.at[d], other) for d, other in enumerate(column_mates)
-    ]
-    unsent.extend(wave_past)
-
-    for copy in loads[3:10]:
-        copy.wait()
-
-    def weigh(i, carry):
-        wr[i] = wr[i] * volume[i]
-        return carry
-
-    lax.fori_loop(0, 125, weigh, 0)
     stiffness()
     for i in range(25):
         face_force[i] = force[i * 5]
     join_radial()
-    lon = lon_out(0)
-
-    for copy in loads[10:]:
-        copy.wait()
+
+    loads[4].wait()
+    for step in range(STEPS):
+        old = [hist[pl.ds(6 - 3 * step + i, 64, 3), :] for i in range(3)]
+        for k in range(3):
+            total = sum(kern[k, i] * old[i] for i in range(3))
+            past[3 * step + k, pl.ds(depth, 1), :] = jnp.sum(total, axis=0, keepdims=True)
+
+    loads[5].wait()
     base = (me["x"] * 16 + me["ylo"]) * 4 + lat
     own = [order[base + 8 * i] for i in range(8)]
     for i in range(8):
@@ -537,25 +555,22 @@
             q8[q, i : i + 1] = cols[own[i], 8 + q : 9 + q]
             gown[q, i : i + 1] = cols[own[i], 11 + q : 12 + q]
 
+    def circle_rows(t, carry):
+        for i in range(8):
+            column = order[((t // 8) * 16 + i * 2 + t // 4 % 2) * 4 + t % 4]
+            for q in range(3):
+                gtt[q, pl.ds(8 * t + i, 1), :] = cols[column, 11 + q : 12 + q]
+        return carry
+
+    lax.fori_loop(0, 32, circle_rows, 0)
+    loads[6].wait()
+
     def take(t, carry):
         for i in range(8):
             lp[t, i : i + 1] = leg[lax.rem(own[i], 128), pl.ds(t, 1), :]
         return carry
 
     lax.fori_loop(0, 40, take, 0)
-    arrived(wave0)
-    wave0 = forward(0)
-
-    lat_copies = lon_in_lat_out(0, lon)
-
-    def circle_row(s, carry):
-        i, rest = s % 8, s // 8
-        column = order[((rest // 8) * 16 + i * 2 + rest // 4 % 2) * 4 + rest % 4]
-        for q in range(3):
-            gtt[q, pl.ds(s, 1), :] = cols[column, 11 + q : 12 + q]
-        return carry
-
-    lax.fori_loop(0, 256, circle_row, 0)
     many = lax.broadcasted_iota(jnp.int32, (256, 128), 1)
     elem = (me["x"] * 2 + me["ylo"]) * 8 + depth
     for a in range(5):
@@ -563,27 +578,50 @@
         gsb[a] = jnp.broadcast_to(jnp.sum(picked, axis=1, keepdims=True), (256, 128))
     for q in range(3):
         ga[128 * q : 128 * q + 128] = jnp.transpose(gtt[q])
-    hist_out[3:63] = hist[0:60]
-    arrived(wave_past)
-
+    loads[3].wait()
+
+    def stack_speed(i):
+        v[i] = stacked(vn, i)
+
+    by_fives(stack_speed)
     offset = [jnp.full((1, 1), x_in[j], jnp.float32) for j in range(3)]
     speed = [jnp.full((1, 1), xv_in[j], jnp.float32) for j in range(3)]
 
+    pl.semaphore_wait(barrier, len(everyone))
+    wave0 = spread(0, 0)
+    halo = halo_out(0)
+    own_past = past.at[:, pl.ds(depth, 1), :]
+    wave_past = [
+        send(own_past, own_past, send_p.at[d], recv_p.at[d], other) for d, other in enumerate(column_mates)
+    ]
+    unsent.extend(wave0)
+    unsent.extend(wave_past)
+    stores = [pltpu.make_async_copy(hist.at[pl.ds(9, 180), :], hist_out.at[pl.ds(9, 180), 0, :], store_sem.at[2])]
+    stores[0].start()
+
+    arrived(wave0)
+    wave0 = forward(0)
+    halo_in(0, halo)
+
+    def invert(i):
+        mass = force[i]
+        inv[i] = 1.0 / jnp.where(even, mass[6:7], mass[7:8])
+
+    def invert_column(i, carry):
+        for b in range(5):
+            invert(25 * i + 5 * b)
+        return carry
+
+    lax.fori_loop(0, 5, invert_column, 0)
+    tail = pack(lambda a, b: inv[(a * 5 + b) * 5], 32)[0] * packing[lat, 2]
+    wave1 = post(1, predicted, tail)
+    arrived(wave_past)
+    by_fives(invert)
     arrived(wave0)
     replies0 = owners(0, analysed(0), offset)
-    lat_in(0, lat_copies)
-
-    def invert(i, carry):
-        mass = force[i]
-        inv[i] = 1.0 / jnp.where(even, mass[6:7], mass[7:8])
-        return carry
-
-    lax.fori_loop(0, 125, invert, 0)
-    tail = pack(lambda a, b: inv[(a * 5 + b) * 5], 32)[0] * packing[lat, 2]
-    wave1 = post(1, predicted, tail)
-    advance()
     arrived(wave1)
     wave1 = forward(1)
+    by_fives(node_step)
     arrived(replies0)
     add_traction(0)
     offset, speed = rigid_step(0, offset, speed)
@@ -592,7 +630,7 @@
     wave2 = post(2, predicted)
     stiffness()
     join_radial()
-    lon = lon_out(1)
+    halo = halo_out(1)
     arrived(wave1)
     factors = g1[1, pl.ds(1, 256, 2), :].reshape(8, 4, 8, 128)
     wide = lax.broadcasted_iota(jnp.int32, (64, 128), 1)
@@ -608,32 +646,44 @@
     replies1 = owners(1, analysed(1) - moved(0), offset)
     arrived(wave2)
     wave2 = forward(2)
-    lat_copies = lon_in_lat_out(1, lon)
-    lat_in(1, lat_copies)
-    advance()
+    inside(node_step)
+    halo_in(1, halo)
+    around(node_step)
     arrived(replies1)
     add_traction(1)
     offset, speed = rigid_step(1, offset, speed)
 
     stiffness()
     join_radial()
-    lon = lon_out(2)
+    halo = halo_out(2)
     shift = moved(1)
     arrived(wave2)
     replies2 = owners(2, analysed(2) - shift, offset)
-    lat_copies = lon_in_lat_out(2, lon)
-    lat_in(2, lat_copies)
-    advance()
+    inside(node_step)
     arrived(replies2)
-    add_traction(2)
+    add_traction(2, shared_moved=False)
     offset, speed = rigid_step(2, offset, speed)
 
-    stores = []
-    for k in range(3):
-        for n, (src, dst) in enumerate(((u, u_out), (v, v_out))):
-            copy = pltpu.make_async_copy(src.at[:, pl.ds(2 * k, 2), :], dst.at[k], store_sem.at[2 * k + n])
-            copy.start()
-            stores.append(copy)
+    def unstack(i):
+        place, speed_now = u[i], v[i]
+        for k in range(3):
+            un[k, i] = place[2 * k : 2 * k + 2]
+            vn[k, i] = speed_now[2 * k : 2 * k + 2]
+
+    inside(unstack)
+    halo_in(2, halo)
+
+    def last_step(i):
+        node_step(i)
+        unstack(i)
+
+    around(last_step)
+    stores.append(pltpu.make_async_copy(hist.at[pl.ds(0, 9), :], hist_out.at[pl.ds(0, 9), 0, :], store_sem.at[3]))
+    stores[1].start()
+    for n, (src, dst) in enumerate(((un, u_out), (vn, v_out))):
+        copy = pltpu.make_async_copy(src, dst, store_sem.at[n])
+        copy.start()
+        stores.append(copy)
     for j in range(3):
         rigid_out[j : j + 1] = jnp.broadcast_to(offset[j], (1, 128))
         rigid_out[3 + j : 4 + j] = jnp.broadcast_to(speed[j], (1, 128))
@@ -641,6 +691,22 @@
     for copy in unsent:
         copy.wait_send()
     for copy in stores:
+        copy.wait()
+
+
+def hand_over(u_in, v_in, hist_in, rigid_in, u_out, v_out, hist_out, x_out, xv_out, u, v, hist, sems):
+    held = ((u_in, u, u_out), (v_in, v, v_out), (hist_in, hist, hist_out))
+    arriving = [pltpu.make_async_copy(src, mid, sems.at[n]) for n, (src, mid, dst) in enumerate(held)]
+    leaving = [pltpu.make_async_copy(mid, dst, sems.at[3 + n]) for n, (src, mid, dst) in enumerate(held)]
+    for copy in arriving:
+        copy.start()
+    for j in range(3):
+        x_out[j] = rigid_in[j, 0]
+        xv_out[j] = rigid_in[3 + j, 0]
+    for first, second in zip(arriving, leaving):
+        first.wait()
+        second.start()
+    for copy in leaving:
         copy.wait()
 
 
@@ -656,34 +722,46 @@
     sem = pltpu.SemaphoreType.DMA
     new_u, new_v, new_history, rigid = pl.pallas_call(
         on_sphere,
-        out_shape=(sds((3, 125, 2, 128)), sds((3, 125, 2, 128)), sds((63, 3, 128)), sds((8, 128))),
-        in_specs=[hbm] * 4 + [smem, vmem, vmem, hbm, hbm, vmem] + [smem] * 3,
-        out_specs=(hbm, hbm, vmem, vmem),
+        out_shape=(sds((3, 125, 2, 128)), sds((3, 125, 2, 128)), sds((189, 1, 128)), sds((8, 128))),
+        in_specs=[hbm] * 4 + [smem, hbm, vmem, hbm, hbm, vmem] + [smem] * 3,
+        out_specs=(hbm, hbm, hbm, vmem),
         scratch_shapes=[
             pltpu.VMEM(shape, jnp.float32)
             for shape in (
-                state, state, state, state, state, (25, 8, 128),
+                (3, 125, 2, 128), (3, 125, 2, 128), (125, 2, 128), (125, 2, 128),
+                state, state, state, state, state, (25, 8, 128), (200, 128),
                 (128, 40, 128), (256, 16, 128), (40, 8, 128), (32, 128), (32, 128), (3, 8, 128), (3, 8, 128),
                 (3, 256, 128), (384, 256), (5, 256, 128), (320, 128), (9, 8, 128), (STEPS + 2, 3, 8, 128),
                 (STEPS, 512, 128), (STEPS, 256, 128),
             )
             + ((STEPS, 25, 8, 128),) * 4
+            + ((STEPS, 4, 5, 8, 128),)
         ]
         + [
-            sem((12,)), sem((6,)), sem((STEPS, 2, GROUP - 1)), sem((STEPS, 2, GROUP - 1)),
-            sem((STEPS, 31)), sem((STEPS, 31)), sem((7,)), sem((7,)), sem((STEPS, 12)), sem((STEPS, 12)),
+            sem((7,)), sem((4,)), sem((STEPS, 2, GROUP - 1)), sem((STEPS, 2, GROUP - 1)),
+            sem((STEPS, 31)), sem((STEPS, 31)), sem((7,)), sem((7,)), sem((STEPS, 16)), sem((STEPS, 16)),
         ],
         compiler_params=pltpu.CompilerParams(
-            collective_id=0, has_side_effects=True, vmem_limit_bytes=40 * 1024 * 1024
+            collective_id=0, has_side_effects=True, vmem_limit_bytes=VMEM_BYTES
         ),
     )(
         displacement.reshape(3, 125, 2, 128), velocity.reshape(3, 125, 2, 128),
         rigidity.reshape(125, 2, 128), density.reshape(125, 2, 128), jnp.asarray(volume),
-        history[0], kernel, jnp.asarray(legendre_table()), jnp.asarray(column_tables()),
+        history.transpose(1, 2, 0, 3).reshape(189, 1, 128), kernel.transpose(1, 2, 0, 3), jnp.asarray(legendre_table()), jnp.asarray(column_tables()),
         jnp.asarray(packed_tables()), owner_order, rigid_offset, rigid_velocity,
     )
+    new_u, new_v, new_history, new_offset, new_speed = pl.pallas_call(
+        hand_over,
+        out_shape=(sds((3, 125, 2, 128)), sds((3, 125, 2, 128)), sds((189, 1, 128)), sds((3,)), sds((3,))),
+        in_specs=[hbm, hbm, hbm, smem],
+        out_specs=(hbm, hbm, hbm, smem, smem),
+        scratch_shapes=[pltpu.VMEM(shape, jnp.float32) for shape in ((3, 125, 2, 128), (3, 125, 2, 128), (189, 1, 128))]
+        + [sem((6,))],
+        compiler_params=pltpu.CompilerParams(vmem_limit_bytes=VMEM_BYTES),
+    )(new_u, new_v, new_history, rigid)
     shape = displacement.shape
-    return new_u.reshape(shape), new_v.reshape(shape), new_history[None], rigid[0:3, 0], rigid[3:6, 0]
+    new_history = new_history.reshape(63, 3, 1, 128).transpose(2, 0, 1, 3)
+    return new_u.reshape(shape), new_v.reshape(shape), new_history, new_offset, new_speed
 
 
 def solution(mesh):

time: 94.4 us -> 75 us (0.79)
  local copies, waits for them, and re-layouts: 15.6 us -> 0 us
  Pallas kernels: 77.8 us -> 74.2 us
    unnamed x27 -> x0, local copies, waits for them, and re-layouts: 14.9 us -> none
    pallas_call x1, Pallas kernels: 77.8 us -> 71 us  [on_device(): pl.pallas_call(on_sphere, out_shape=(sds((3, 125, 2, 128)), sds((3, 125,...]
    pallas_call x0 -> x1, Pallas kernels: none -> 3.19 us  [on_device(): pl.pallas_call(hand_over, out_shape=(sds((3, 125, 2, 128)), sds((3, 125,...]
where the time goes in v3:
time: 75 us; the launch traced here: 74.8 us
  Pallas kernels  74.2 us (99%)
    pallas_call x1, Pallas kernels, on_device(): pl.pallas_call(on_sphere, out_shape=(sds((3, 125, 2, 128)), sds((3, 125,...  71 us
    pallas_call x1, Pallas kernels, on_device(): pl.pallas_call(hand_over, out_shape=(sds((3, 125, 2, 128)), sds((3, 125,...  3.19 us

profile of v3, /device:TPU:1, one launch (start us, length us, event | category | flops | bytes accessed | tf_op | source)
XLA Modules:
  0.0 74.8 jit_solution(1730691056677595651)
XLA Ops:
  0.6 71.0 %shard_map.164 = (f32[3,125,2,128]{3,2,1,0:T(2,128)}, f32[3,125,2,128]{3,2,1,0:T(2,128)}, f32[189,1,128]{2,1,0:T(1,128)}, f32[8,128]{1,0:T(8,128)}) custom-call(f32[3,125,2,128]{3,2,1,0:T(2,128)} %bitcast.13, f32[3,125,2,128]{3,2,1,0:T(2,128)} %bitcast.14, f32[125,2,128]{2,1,0:T(2,128)} %bitcast.16, f32[125,2,128]{2,1,0:T(2,128)} %bitcast.17, ...), custom_call_target="tpu_custom_call" | custom-call | tf_op jit(solution)/shard_map/pallas_call | solution.py:723
  71.6 3.2 %shard_map.165 = (f32[3,125,2,128]{3,2,1,0:T(2,128)}, f32[3,125,2,128]{3,2,1,0:T(2,128)}, f32[189,1,128]{2,1,0:T(1,128)}, f32[3]{0:T(128)}, f32[3]{0:T(128)}) custom-call(f32[3,125,2,128]{3,2,1,0:T(2,128)} %get-tuple-element.14.u_in, f32[3,125,2,128]{3,2,1,0:T(2,128)} %get-tuple-element.15.v_in, f32[189,1,128]{2,1,0:T(1,128)} %get-tuple-element.16.hist_in, ...), custom_call_target="tpu_custom_call" | custom-call | tf_op jit(solution)/shard_map/pallas_call | solution.py:753

commit v4 on v3

--- a/solution.py
+++ b/solution.py
@@ -186,7 +186,7 @@
     u_in, v_in, rig_in, den_in, volume, hist_in, kern, leg_in, cols_in, packing, order, x_in, xv_in,
     u_out, v_out, hist_out, rigid_out,
     un, vn, rn, dn, u, v, wr, force, inv, face_force, hist, leg, cols, lp, e32, d32, q8, gown, gtt, ga, gsb, wi, past, coefs, g1, g2,
-    lon_lo, lon_hi, lat_lo, lat_hi, edges,
+    lon_lo, lon_hi, lat_lo, lat_hi, edges, pack_up, pack_down,
     load_sem, store_sem, send1, recv1, send2, recv2, send_p, recv_p, send_h, recv_h,
 ):
     me = {axis: lax.axis_index(axis) for axis in AXES}
@@ -350,40 +350,87 @@
             force[i * 5] = low + jnp.where(lanes == 0, 0.0, pltpu.roll(high, 1, 1))
             force[i * 5 + 4] = high + jnp.where(lanes == 127, 0.0, pltpu.roll(low, 127, 1))
 
+    pairs = [(n, 2 * n, min(2 * n + 1, 24)) for n in range(13)]
+    not_last, not_first = lat < 3, lat > 0
+
     def halo_out(step):
-        moves = [
-            (pl.ds(100, 25), lon_lo.at[step], lon_next),
-            (pl.ds(0, 25), lon_hi.at[step], lon_prev),
-            (pl.ds(120, 5), edges.at[step, 0], corners[0]),
-            (pl.ds(100, 5), edges.at[step, 1], corners[1]),
-            (pl.ds(20, 5), edges.at[step, 2], corners[2]),
-            (pl.ds(0, 5), edges.at[step, 3], corners[3]),
+        lon_copies = [
+            send(force.at[pl.ds(100, 25)], lon_lo.at[step], send_h.at[step, 0], recv_h.at[step, 0], lon_next),
+            send(force.at[pl.ds(0, 25)], lon_hi.at[step], send_h.at[step, 1], recv_h.at[step, 1], lon_prev),
         ]
-        for a in range(5):
-            moves.append((pl.ds(25 * a + 20, 5), lat_lo.at[step, pl.ds(5 * a, 5)], lat_next))
-            moves.append((pl.ds(25 * a, 5), lat_hi.at[step, pl.ds(5 * a, 5)], lat_prev))
-        return [
-            send(force.at[rows], dst, send_h.at[step, n], recv_h.at[step, n], other)
-            for n, (rows, dst, other) in enumerate(moves)
-        ]
+        for n, one, two in pairs:
+            up = [force[25 * (x // 5) + 20 + x % 5] for x in (one, two)]
+            down = [force[25 * (x // 5) + x % 5] for x in (one, two)]
+            pack_up[n] = jnp.where(even, pltpu.roll(up[1], 7, 0), up[0])
+            pack_down[n] = jnp.where(even, down[0], pltpu.roll(down[1], 1, 0))
+
+        def moves(packed, face, beside, edge):
+            return [
+                pltpu.make_async_remote_copy(
+                    src_ref=packed.at[pl.ds(start, count)], dst_ref=dst, send_sem=send_h.at[step, at],
+                    recv_sem=recv_h.at[step, at], device_id=other, device_id_type=MESH_ID,
+                )
+                for start, count, dst, at, other in (
+                    (0, 13, face.at[step], 2 + edge, beside),
+                    (10, 3, edges.at[step, edge], 4 + edge, corners[edge]),
+                    (0, 3, edges.at[step, 2 + edge], 6 + edge, corners[2 + edge]),
+                )
+            ]
+
+        rising = moves(pack_up, lat_lo, lat_next, 0)
+        falling = moves(pack_down, lat_hi, lat_prev, 1)
+
+        @pl.when(not_last)
+        def _():
+            for copy in rising:
+                copy.start()
+
+        @pl.when(not_first)
+        def _():
+            for copy in falling:
+                copy.start()
+
+        return lon_copies, rising, falling
 
     def halo_in(step, copies):
-        for copy in copies:
+        lon_copies, rising, falling = copies
+        for copy in lon_copies:
             copy.wait()
+
+        @pl.when(not_last)
+        def _():
+            for copy in rising:
+                copy.wait_send()
+            for copy in falling:
+                copy.wait_recv()
+
+        @pl.when(not_first)
+        def _():
+            for copy in falling:
+                copy.wait_send()
+            for copy in rising:
+                copy.wait_recv()
+
         force[0:25] = force[0:25] + lon_lo[step]
         force[100:125] = force[100:125] + lon_hi[step]
-        for a in range(5):
-            for c in range(5):
-                low, high = force[a * 25 + c], force[a * 25 + 20 + c]
-                below, above = lat_lo[step, a * 5 + c], lat_hi[step, a * 5 + c]
-                if a == 0:
-                    below, above = below + edges[step, 0, c], above + edges[step, 1, c]
-                if a == 4:
-                    below, above = below + edges[step, 2, c], above + edges[step, 3, c]
-                below = jnp.where(lat == 0, 0.0, pltpu.roll(below, 7, 0))
-                above = jnp.where(lat == 3, 0.0, pltpu.roll(above, 1, 0))
-                force[a * 25 + c] = low + jnp.where(even, below, pltpu.roll(high, 1, 0))
-                force[a * 25 + 20 + c] = high + jnp.where(even, pltpu.roll(low, 7, 0), above)
+        for n, one, two in pairs:
+            below, above = lat_lo[step, n], lat_hi[step, n]
+            if n <= 2:
+                first, second = edges[step, 0, n], edges[step, 1, n]
+                if n == 2:
+                    first, second = jnp.where(even, 0.0, first), jnp.where(even, second, 0.0)
+                below, above = below + first, above + second
+            if n >= 10:
+                below, above = below + edges[step, 2, n - 10], above + edges[step, 3, n - 10]
+            below = jnp.where(not_first, below, 0.0)
+            above = jnp.where(not_last, above, 0.0)
+            for x, part_below, part_above in (
+                (one, pltpu.roll(below, 7, 0), pltpu.roll(above, 1, 0)),
+                (two, below, above),
+            )[: 1 if one == two else 2]:
+                low, high = force[25 * (x // 5) + x % 5], force[25 * (x // 5) + 20 + x % 5]
+                force[25 * (x // 5) + x % 5] = low + jnp.where(even, part_below, pltpu.roll(high, 1, 0))
+                force[25 * (x // 5) + 20 + x % 5] = high + jnp.where(even, pltpu.roll(low, 7, 0), part_above)
 
     def node_step(i):
         speed_now = jnp.where(in_field, v[i] + time_step * (force[i] * inv[i]), 0.0)
@@ -734,12 +781,13 @@
                 (3, 256, 128), (384, 256), (5, 256, 128), (320, 128), (9, 8, 128), (STEPS + 2, 3, 8, 128),
                 (STEPS, 512, 128), (STEPS, 256, 128),
             )
-            + ((STEPS, 25, 8, 128),) * 4
-            + ((STEPS, 4, 5, 8, 128),)
+            + ((STEPS, 25, 8, 128),) * 2
+            + ((STEPS, 13, 8, 128),) * 2
+            + ((STEPS, 4, 3, 8, 128), (13, 8, 128), (13, 8, 128))
         ]
         + [
             sem((7,)), sem((4,)), sem((STEPS, 2, GROUP - 1)), sem((STEPS, 2, GROUP - 1)),
-            sem((STEPS, 31)), sem((STEPS, 31)), sem((7,)), sem((7,)), sem((STEPS, 16)), sem((STEPS, 16)),
+            sem((STEPS, 31)), sem((STEPS, 31)), sem((7,)), sem((7,)), sem((STEPS, 8)), sem((STEPS, 8)),
         ],
         compiler_params=pltpu.CompilerParams(
             collective_id=0, has_side_effects=True, vmem_limit_bytes=VMEM_BYTES

time: 75 us -> 69.3 us (0.924)
  Pallas kernels: 74.2 us -> 68.5 us
    pallas_call x1, Pallas kernels: 71 us -> 65.3 us  [on_device(): pl.pallas_call(on_sphere, out_shape=(sds((3, 125, 2, 128)), sds((3, 125,...]
where the time goes in v4:
time: 69.3 us; the launch traced here: 69.1 us
  Pallas kernels  68.5 us (99%)
    pallas_call x1, Pallas kernels, on_device(): pl.pallas_call(on_sphere, out_shape=(sds((3, 125, 2, 128)), sds((3, 125,...  65.3 us
    pallas_call x1, Pallas kernels, on_device(): pl.pallas_call(hand_over, out_shape=(sds((3, 125, 2, 128)), sds((3, 125,...  3.19 us

profile of v4, /device:TPU:1, one launch (start us, length us, event | category | flops | bytes accessed | tf_op | source)
XLA Modules:
  0.0 69.1 jit_solution(17460739244235378083)
XLA Ops:
  0.6 65.3 %shard_map.164 = (f32[3,125,2,128]{3,2,1,0:T(2,128)}, f32[3,125,2,128]{3,2,1,0:T(2,128)}, f32[189,1,128]{2,1,0:T(1,128)}, f32[8,128]{1,0:T(8,128)}) custom-call(f32[3,125,2,128]{3,2,1,0:T(2,128)} %bitcast.13, f32[3,125,2,128]{3,2,1,0:T(2,128)} %bitcast.14, f32[125,2,128]{2,1,0:T(2,128)} %bitcast.16, f32[125,2,128]{2,1,0:T(2,128)} %bitcast.17, ...), custom_call_target="tpu_custom_call" | custom-call | tf_op jit(solution)/shard_map/pallas_call | solution.py:770
  65.9 3.2 %shard_map.165 = (f32[3,125,2,128]{3,2,1,0:T(2,128)}, f32[3,125,2,128]{3,2,1,0:T(2,128)}, f32[189,1,128]{2,1,0:T(1,128)}, f32[3]{0:T(128)}, f32[3]{0:T(128)}) custom-call(f32[3,125,2,128]{3,2,1,0:T(2,128)} %get-tuple-element.14.u_in, f32[3,125,2,128]{3,2,1,0:T(2,128)} %get-tuple-element.15.v_in, f32[189,1,128]{2,1,0:T(1,128)} %get-tuple-element.16.hist_in, ...), custom_call_target="tpu_custom_call" | custom-call | tf_op jit(solution)/shard_map/pallas_call | solution.py:801

commit v5 on v4

--- a/solution.py
+++ b/solution.py
@@ -186,7 +186,7 @@
     u_in, v_in, rig_in, den_in, volume, hist_in, kern, leg_in, cols_in, packing, order, x_in, xv_in,
     u_out, v_out, hist_out, rigid_out,
     un, vn, rn, dn, u, v, wr, force, inv, face_force, hist, leg, cols, lp, e32, d32, q8, gown, gtt, ga, gsb, wi, past, coefs, g1, g2,
-    lon_lo, lon_hi, lat_lo, lat_hi, edges, pack_up, pack_down,
+    lon_lo, lon_hi, lat_lo, lat_hi, edges, pack_up, pack_down, close_up, close_down,
     load_sem, store_sem, send1, recv1, send2, recv2, send_p, recv_p, send_h, recv_h,
 ):
     me = {axis: lax.axis_index(axis) for axis in AXES}
@@ -326,24 +326,6 @@
         along(5, lambda i: (i // 5) * 25 + i % 5, False)
         along(1, lambda i: i * 5, False)
 
-    def interface_stiffness():
-        def radial(i, carry):
-            grads, weights = gradients(i * 5, 1)
-            face_force[i] = -divergence(grads, 0)
-            return carry
-
-        def flat_lines(i, carry):
-            grads, weights = gradients(i * 5, 25)
-            for q in range(5):
-                face_force[q * 5 + i] = face_force[q * 5 + i] - divergence(grads, q)
-            grads, weights = gradients(i * 25, 5)
-            for q in range(5):
-                face_force[i * 5 + q] = face_force[i * 5 + q] - divergence(grads, q)
-            return carry
-
-        lax.fori_loop(0, 25, radial, 0)
-        lax.fori_loop(0, 5, flat_lines, 0)
-
     def join_radial():
         for i in range(25):
             low, high = force[i * 5], force[i * 5 + 4]
@@ -353,10 +335,38 @@
     pairs = [(n, 2 * n, min(2 * n + 1, 24)) for n in range(13)]
     not_last, not_first = lat < 3, lat > 0
 
+    def close_pack(base, packed):
+        last = jnp.zeros((8, 128), jnp.float32)
+        for b in range(5):
+            third = force[base + 5 * b + 3]
+            for c in range(3):
+                packed[3 * b + c] = jnp.where(in_field, force[base + 5 * b + c], pltpu.roll(third, 6 - 2 * c, 0))
+            last = jnp.where(lanes == b, jnp.broadcast_to(force[base + 5 * b + 4][:, 127:128], (8, 128)), last)
+        packed[15] = last
+
+    def close_add(base, packed):
+        last = packed[15]
+        for b in range(5):
+            parts = [packed[3 * b + c] for c in range(3)]
+            third = jnp.where(subs < 2, pltpu.roll(parts[0], 2, 0), pltpu.roll(parts[1], 4, 0))
+            third = jnp.where(subs < 4, third, pltpu.roll(parts[2], 6, 0))
+            end = jnp.where(lanes == 127, last[:, b : b + 1], pltpu.roll(parts[0], 127, 1))
+            for c, part in enumerate(parts + [third, end]):
+                at = base + 5 * b + c
+                force[at] = force[at] + jnp.where(in_field, part, 0.0)
+
     def halo_out(step):
+        if step == 0:
+            faces = [force.at[pl.ds(100, 25)], force.at[pl.ds(0, 25)]]
+            into = [lon_lo.at[0], lon_hi.at[0]]
+        else:
+            close_pack(100, close_up)
+            close_pack(0, close_down)
+            faces = [close_up, close_down]
+            into = [lon_lo.at[step, pl.ds(0, 16)], lon_hi.at[step, pl.ds(0, 16)]]
         lon_copies = [
-            send(force.at[pl.ds(100, 25)], lon_lo.at[step], send_h.at[step, 0], recv_h.at[step, 0], lon_next),
-            send(force.at[pl.ds(0, 25)], lon_hi.at[step], send_h.at[step, 1], recv_h.at[step, 1], lon_prev),
+            send(faces[n], into[n], send_h.at[step, n], recv_h.at[step, n], other)
+            for n, other in enumerate((lon_next, lon_prev))
         ]
         for n, one, two in pairs:
             up = [force[25 * (x // 5) + 20 + x % 5] for x in (one, two)]
@@ -411,8 +421,12 @@
             for copy in rising:
                 copy.wait_recv()
 
-        force[0:25] = force[0:25] + lon_lo[step]
-        force[100:125] = force[100:125] + lon_hi[step]
+        if step == 0:
+            force[0:25] = force[0:25] + lon_lo[0]
+            force[100:125] = force[100:125] + lon_hi[0]
+        else:
+            close_add(0, lon_lo.at[step])
+            close_add(100, lon_hi.at[step])
         for n, one, two in pairs:
             below, above = lat_lo[step, n], lat_hi[step, n]
             if n <= 2:
@@ -673,11 +687,12 @@
     add_traction(0)
     offset, speed = rigid_step(0, offset, speed)
 
-    interface_stiffness()
-    wave2 = post(2, predicted)
     stiffness()
+    for i in range(25):
+        face_force[i] = force[i * 5]
     join_radial()
     halo = halo_out(1)
+    wave2 = post(2, predicted)
     arrived(wave1)
     factors = g1[1, pl.ds(1, 256, 2), :].reshape(8, 4, 8, 128)
     wide = lax.broadcasted_iota(jnp.int32, (64, 128), 1)
@@ -783,7 +798,7 @@
             )
             + ((STEPS, 25, 8, 128),) * 2
             + ((STEPS, 13, 8, 128),) * 2
-            + ((STEPS, 4, 3, 8, 128), (13, 8, 128), (13, 8, 128))
+            + ((STEPS, 4, 3, 8, 128), (13, 8, 128), (13, 8, 128), (16, 8, 128), (16, 8, 128))
         ]
         + [
             sem((7,)), sem((4,)), sem((STEPS, 2, GROUP - 1)), sem((STEPS, 2, GROUP - 1)),

time: 69.3 us -> 64.9 us (0.937)
  Pallas kernels: 68.5 us -> 64.1 us
    pallas_call x1, Pallas kernels: 65.3 us -> 60.9 us  [on_device(): pl.pallas_call(on_sphere, out_shape=(sds((3, 125, 2, 128)), sds((3, 125,...]
where the time goes in v5:
time: 64.9 us; the launch traced here: 64.7 us
  Pallas kernels  64.1 us (99%)
    pallas_call x1, Pallas kernels, on_device(): pl.pallas_call(on_sphere, out_shape=(sds((3, 125, 2, 128)), sds((3, 125,...  60.9 us
    pallas_call x1, Pallas kernels, on_device(): pl.pallas_call(hand_over, out_shape=(sds((3, 125, 2, 128)), sds((3, 125,...  3.19 us

profile of v5, /device:TPU:1, one launch (start us, length us, event | category | flops | bytes accessed | tf_op | source)
XLA Modules:
  0.0 64.7 jit_solution(7352555144898017576)
XLA Ops:
  0.6 60.9 %shard_map.164 = (f32[3,125,2,128]{3,2,1,0:T(2,128)}, f32[3,125,2,128]{3,2,1,0:T(2,128)}, f32[189,1,128]{2,1,0:T(1,128)}, f32[8,128]{1,0:T(8,128)}) custom-call(f32[3,125,2,128]{3,2,1,0:T(2,128)} %bitcast.13, f32[3,125,2,128]{3,2,1,0:T(2,128)} %bitcast.14, f32[125,2,128]{2,1,0:T(2,128)} %bitcast.16, f32[125,2,128]{2,1,0:T(2,128)} %bitcast.17, ...), custom_call_target="tpu_custom_call" | custom-call | tf_op jit(solution)/shard_map/pallas_call | solution.py:785
  61.5 3.2 %shard_map.165 = (f32[3,125,2,128]{3,2,1,0:T(2,128)}, f32[3,125,2,128]{3,2,1,0:T(2,128)}, f32[189,1,128]{2,1,0:T(1,128)}, f32[3]{0:T(128)}, f32[3]{0:T(128)}) custom-call(f32[3,125,2,128]{3,2,1,0:T(2,128)} %get-tuple-element.14.u_in, f32[3,125,2,128]{3,2,1,0:T(2,128)} %get-tuple-element.15.v_in, f32[189,1,128]{2,1,0:T(1,128)} %get-tuple-element.16.hist_in, ...), custom_call_target="tpu_custom_call" | custom-call | tf_op jit(solution)/shard_map/pallas_call | solution.py:816

commit v6 on v5

--- a/solution.py
+++ b/solution.py
@@ -1,4 +1,5 @@
 import functools
+import itertools
 import math
 
 import jax
@@ -182,6 +183,21 @@
     return found
 
 
+def farthest_first(axes, me):
+    shifts = []
+    for shift in itertools.product(*(range(SIZES[axis]) for axis in axes)):
+        by = dict(zip(axes, shift))
+        hops = sum(min(by.get(axis, 0), SIZES[axis] - by.get(axis, 0)) for axis in ("x", "z"))
+        hops += (0, 1, 2, 1)[2 * by.get("yhi", 0) + by.get("ylo", 0)]
+        if any(shift):
+            shifts.append((-hops, shift))
+    found = []
+    for hops, shift in sorted(shifts):
+        other = {**me, **{axis: lax.rem(me[axis] + by, SIZES[axis]) for axis, by in zip(axes, shift)}}
+        found.append(tuple(other[axis] for axis in AXES))
+    return found
+
+
 def on_sphere(
     u_in, v_in, rig_in, den_in, volume, hist_in, kern, leg_in, cols_in, packing, order, x_in, xv_in,
     u_out, v_out, hist_out, rigid_out,
@@ -191,9 +207,9 @@
 ):
     me = {axis: lax.axis_index(axis) for axis in AXES}
     lat, depth = flat(LAT, me), me["z"]
-    near = partners(FIRST, me, range(1, GROUP))
-    far = partners(SECOND, me, range(1, GROUP))
-    plane = partners(PLANE, me, range(1, 32))
+    near = farthest_first(FIRST, me)
+    far = farthest_first(SECOND, me)
+    plane = farthest_first(PLANE, me)
     column_mates = partners(("z",), me, range(1, 8))
     lon_next, lon_prev = partners(BLK, me, (1, -1))
     lat_next, lat_prev = partners(LAT, me, (1, -1))

time: 64.9 us -> 62.5 us (0.963)
  Pallas kernels: 64.1 us -> 61.7 us
    pallas_call x1, Pallas kernels: 60.9 us -> 58.5 us  [on_device(): pl.pallas_call(on_sphere, out_shape=(sds((3, 125, 2, 128)), sds((3, 125,...]
where the time goes in v6:
time: 62.5 us; the launch traced here: 62.4 us
  Pallas kernels  61.7 us (99%)
  between operations  0.64 us (1%)
    pallas_call x1, Pallas kernels, on_device(): pl.pallas_call(on_sphere, out_shape=(sds((3, 125, 2, 128)), sds((3, 125,...  58.5 us
    pallas_call x1, Pallas kernels, on_device(): pl.pallas_call(hand_over, out_shape=(sds((3, 125, 2, 128)), sds((3, 125,...  3.19 us

profile of v6, /device:TPU:1, one launch (start us, length us, event | category | flops | bytes accessed | tf_op | source)
XLA Modules:
  0.0 62.4 jit_solution(12012163349659821814)
XLA Ops:
  0.6 58.5 %shard_map.164 = (f32[3,125,2,128]{3,2,1,0:T(2,128)}, f32[3,125,2,128]{3,2,1,0:T(2,128)}, f32[189,1,128]{2,1,0:T(1,128)}, f32[8,128]{1,0:T(8,128)}) custom-call(f32[3,125,2,128]{3,2,1,0:T(2,128)} %bitcast.13, f32[3,125,2,128]{3,2,1,0:T(2,128)} %bitcast.14, f32[125,2,128]{2,1,0:T(2,128)} %bitcast.16, f32[125,2,128]{2,1,0:T(2,128)} %bitcast.17, ...), custom_call_target="tpu_custom_call" | custom-call | tf_op jit(solution)/shard_map/pallas_call | solution.py:801
  59.2 3.2 %shard_map.165 = (f32[3,125,2,128]{3,2,1,0:T(2,128)}, f32[3,125,2,128]{3,2,1,0:T(2,128)}, f32[189,1,128]{2,1,0:T(1,128)}, f32[3]{0:T(128)}, f32[3]{0:T(128)}) custom-call(f32[3,125,2,128]{3,2,1,0:T(2,128)} %get-tuple-element.14.u_in, f32[3,125,2,128]{3,2,1,0:T(2,128)} %get-tuple-element.15.v_in, f32[189,1,128]{2,1,0:T(1,128)} %get-tuple-element.16.hist_in, ...), custom_call_target="tpu_custom_call" | custom-call | tf_op jit(solution)/shard_map/pallas_call | solution.py:832

commit v7 on v6

--- a/solution.py
+++ b/solution.py
@@ -214,7 +214,7 @@
     lon_next, lon_prev = partners(BLK, me, (1, -1))
     lat_next, lat_prev = partners(LAT, me, (1, -1))
     corners = [lon[:3] + colat[3:] for lon in (lon_next, lon_prev) for colat in (lat_next, lat_prev)]
-    everyone = near + plane + [lon_next, lon_prev, lat_next, lat_prev] + corners
+    everyone = corners + [lon_next, lon_prev, lat_next, lat_prev] + plane + near
     barrier = pltpu.get_barrier_semaphore()
     for other in everyone:
         pl.semaphore_signal(barrier, inc=1, device_id=other, device_id_type=MESH_ID)

time: 62.5 us -> 62.5 us (level)
  no operation moved by 1% of the time
where the time goes in v7:
time: 62.5 us; the launch traced here: 62.4 us
  Pallas kernels  61.7 us (99%)
  between operations  0.64 us (1%)
    pallas_call x1, Pallas kernels, on_device(): pl.pallas_call(on_sphere, out_shape=(sds((3, 125, 2, 128)), sds((3, 125,...  58.5 us
    pallas_call x1, Pallas kernels, on_device(): pl.pallas_call(hand_over, out_shape=(sds((3, 125, 2, 128)), sds((3, 125,...  3.19 us

profile of v7, /device:TPU:1, one launch (start us, length us, event | category | flops | bytes accessed | tf_op | source)
XLA Modules:
  0.0 62.4 jit_solution(10919269511622650770)
XLA Ops:
  0.6 58.5 %shard_map.164 = (f32[3,125,2,128]{3,2,1,0:T(2,128)}, f32[3,125,2,128]{3,2,1,0:T(2,128)}, f32[189,1,128]{2,1,0:T(1,128)}, f32[8,128]{1,0:T(8,128)}) custom-call(f32[3,125,2,128]{3,2,1,0:T(2,128)} %bitcast.13, f32[3,125,2,128]{3,2,1,0:T(2,128)} %bitcast.14, f32[125,2,128]{2,1,0:T(2,128)} %bitcast.16, f32[125,2,128]{2,1,0:T(2,128)} %bitcast.17, ...), custom_call_target="tpu_custom_call" | custom-call | tf_op jit(solution)/shard_map/pallas_call | solution.py:801
  59.2 3.2 %shard_map.165 = (f32[3,125,2,128]{3,2,1,0:T(2,128)}, f32[3,125,2,128]{3,2,1,0:T(2,128)}, f32[189,1,128]{2,1,0:T(1,128)}, f32[3]{0:T(128)}, f32[3]{0:T(128)}) custom-call(f32[3,125,2,128]{3,2,1,0:T(2,128)} %get-tuple-element.14.u_in, f32[3,125,2,128]{3,2,1,0:T(2,128)} %get-tuple-element.15.v_in, f32[189,1,128]{2,1,0:T(1,128)} %get-tuple-element.16.hist_in, ...), custom_call_target="tpu_custom_call" | custom-call | tf_op jit(solution)/shard_map/pallas_call | solution.py:832
